TPU v7x, 256 devices: a whole 4x4x8 slice. The times are simulated.
256 devices in a mesh: row: 16 (over x_lo, z), col: 16 (over y, x_hi, core).
Axes of the slice: x: 4 (x_hi: 2, x_lo: 2; x = x_hi * 2 + x_lo), y: 4, z: 8, core: 2. Of those that a mesh axis runs over, the one named last changes fastest.
Arguments:
- grad_out: bfloat16 [512, 12288], P('row', 'col'), may hold values from -6 to 6
- pre_act: bfloat16 [512, 49152], P(None, 'row'), may hold values from -6 to 6
- weight: bfloat16 [49152, 12288], P('row', 'col'), may hold values from -0.02734375 to 0.02734375
Outputs:
- grad_pre: bfloat16 [512, 49152], P('col', 'row')
- grad_weight: bfloat16 [49152, 12288], P('row', 'col')
All inputs are finite; a program needn't handle non-finite values.
Results may differ from a plain program's by a relative error of at most 0.022.
Values may be sent and summed in bfloat16 or wider, within the bound.
A program may use at most 64 MiB of HBM per device.

v0:
```python
import jax
import jax.numpy as jnp
from jax import lax
from jax.sharding import PartitionSpec as P


def from_behind(block, axis, distance):
    devices = range(lax.axis_size(axis))
    route = [((i - distance) % len(devices), i) for i in devices]
    return lax.ppermute(block, axis, route)


def gelu_value(values):
    inner = 0.7978845608 * (values + 0.044715 * values * values * values)
    return 0.5 * values * (1.0 + jnp.tanh(inner))


def gelu_slope(values):
    inner = 0.7978845608 * (values + 0.044715 * values * values * values)
    tanh_value = jnp.tanh(inner)
    return 0.5 * (1.0 + tanh_value) + 0.5 * values * (
        1.0 - tanh_value * tanh_value
    ) * 0.7978845608 * (1.0 + 3.0 * 0.044715 * values * values)


def body(grad_out, pre_act, weight):
    row_block = grad_out.shape[0]
    width_cols = grad_out.shape[1]
    token_rows = pre_act.shape[0]
    hidden_cols = weight.shape[0]
    row_count = lax.axis_size("row")
    col_count = lax.axis_size("col")
    row_index = lax.axis_index("row")
    col_index = lax.axis_index("col")
    activation = gelu_value(pre_act.astype(jnp.float32)).astype(jnp.bfloat16)

    def record(partial_value, collected, current, anchor):
        product = lax.dot_general(
            current, weight, (((1,), (1,)), ((), ())), preferred_element_type=jnp.float32
        )
        offset = anchor * row_block
        partial_value = lax.dynamic_update_slice_in_dim(
            partial_value, product.astype(jnp.bfloat16), offset, 0
        )
        collected = lax.dynamic_update_slice_in_dim(collected, current, offset, 0)
        return (partial_value, collected)

    partial_value = jnp.zeros((token_rows, hidden_cols), jnp.bfloat16)
    collected = jnp.zeros((token_rows, width_cols), jnp.bfloat16)
    partial_value, collected = record(partial_value, collected, grad_out, row_index)

    def one_step(step, state_tuple):
        current, partial_value, collected = state_tuple
        current = from_behind(current, "row", 1)
        partial_value, collected = record(
            partial_value, collected, current, (row_index - step) % row_count
        )
        return (current, partial_value, collected)

    current, partial_value, collected = lax.fori_loop(
        1, row_count, one_step, (grad_out, partial_value, collected)
    )
    grad_weight = lax.dot_general(
        activation, collected, (((0,), (0,)), ((), ())), preferred_element_type=jnp.float32
    ).astype(jnp.bfloat16)
    owned_rows = token_rows // col_count
    stacked = partial_value.reshape(col_count, owned_rows, hidden_cols)
    running = lax.dynamic_index_in_dim(
        stacked, (col_index - 1) % col_count, 0, keepdims=False
    ).astype(jnp.float32)

    def chain_step(step, running):
        arrived = from_behind(running.astype(jnp.bfloat16), "col", 1).astype(running.dtype)
        local_tile = lax.dynamic_index_in_dim(
            stacked, (col_index - 1 - step) % col_count, 0, keepdims=False
        )
        return arrived + local_tile.astype(jnp.float32)

    summed = lax.fori_loop(1, col_count, chain_step, running)
    own_rows = lax.dynamic_slice_in_dim(pre_act, col_index * owned_rows, owned_rows, 0)
    grad_pre = (summed * gelu_slope(own_rows.astype(jnp.float32))).astype(jnp.bfloat16)
    return (grad_pre, grad_weight)


def solution(mesh):
    placed = (P("row", "col"), P(None, "row"), P("row", "col"))
    return jax.shard_map(
        body,
        mesh=mesh,
        in_specs=placed,
        out_specs=(P("col", "row"), P("row", "col")),
        check_vma=False,
    )
```

profile of v0, /device:TPU:2, one launch (start us, length us, event | category | flops | bytes accessed | tf_op | source)
XLA Modules:
  0.0 347.7 jit_solution(15573135003116366130)
XLA Ops:
  1.8 3.8 %fusion.6 = bf16[512,3072]{1,0:T(8,128)(2,1)S(1)} fusion(bf16[512,3072]{1,0:T(8,128)(2,1)S(1)} %broadcast_in_dim.6, s32[]{:T(128)S(6)} %select_n.73, bf16[32,768]{1,0:T(8,128)(2,1)S(1)} %copy.28, bf16[3072,768]{1,0:T(8,128)(2,1)} %param.9), kind=kOutput, calls=%fused_computation.16 | convolution fusion | flops 151093248 | bytes 4964356 | tf_op jit(solution)/shard_map/dot_general | solution.py:38
  6.6 162.0 %while.34 = (s32[]{:T(128)}, bf16[32,768]{1,0:T(8,128)(2,1)S(1)}, bf16[512,3072]{1,0:T(8,128)(2,1)S(1)}, bf16[512,768]{1,0:T(8,128)(2,1)}, bf16[3072,768]{1,0:T(...) while((s32[]{:T(128)}, bf16[32,768]{1,0:T(8,128)(2,1)S(1)}, ...), condition=%wide.region_1.2_spmd, body=%wide.region_0.1_spmd.sunk | while | flops 151093264 | bytes 5357900 | solution.py:60
  8.5 6.0 %collective-permute-done = bf16[32,768]{1,0:T(8,128)(2,1)S(1)} collective-permute-done((bf16[32,768]{1,0:T(8,128)(2,1)S(1)}, bf16[32,768]{1,0:T(8,128)(2,1)S(1)}, u32[]{:S(2)}, u32[]{:S(2)}) %collective-permute-start) | collective-permute-done | bytes 49184 | tf_op jit(solution)/shard_map/while/body/eval_jaxpr/ppermute | solution.py:10
  15.1 3.8 %fusion.35 = bf16[512,3072]{1,0:T(8,128)(2,1)S(1)} fusion(bf16[512,3072]{1,0:T(8,128)(2,1)S(1)} %get-tuple-element.371, s32[]{:T(128)S(6)} %select_n.82, bf16[32,768]{1,0:T(8,128)(2,1)S(1)} %collective-permute-done, bf16[3072,768]{1,0:T(8,128)(2,1)} %get-tuple-element.385), kind=kOutput, calls=%fused_computation.1.clone.1 | convolution fusion | flops 151093248 | bytes 4964356 | tf_op jit(solution)/shard_map/while/body/eval_jaxpr/dot_general | solution.py:38
  19.0 6.2 %collective-permute-done = bf16[32,768]{1,0:T(8,128)(2,1)S(1)} collective-permute-done((bf16[32,768]{1,0:T(8,128)(2,1)S(1)}, bf16[32,768]{1,0:T(8,128)(2,1)S(1)}, u32[]{:S(2)}, u32[]{:S(2)}) %collective-permute-start) | collective-permute-done | bytes 49184 | tf_op jit(solution)/shard_map/while/body/eval_jaxpr/ppermute | solution.py:10
  29.7 6.2 %collective-permute-done = bf16[32,768]{1,0:T(8,128)(2,1)S(1)} collective-permute-done((bf16[32,768]{1,0:T(8,128)(2,1)S(1)}, bf16[32,768]{1,0:T(8,128)(2,1)S(1)}, u32[]{:S(2)}, u32[]{:S(2)}) %collective-permute-start) | collective-permute-done | bytes 49184 | tf_op jit(solution)/shard_map/while/body/eval_jaxpr/ppermute | solution.py:10
  36.5 3.8 %fusion.35 = bf16[512,3072]{1,0:T(8,128)(2,1)S(1)} fusion(bf16[512,3072]{1,0:T(8,128)(2,1)S(1)} %get-tuple-element.371, s32[]{:T(128)S(6)} %select_n.82, bf16[32,768]{1,0:T(8,128)(2,1)S(1)} %collective-permute-done, bf16[3072,768]{1,0:T(8,128)(2,1)} %get-tuple-element.385), kind=kOutput, calls=%fused_computation.1.clone.1 | convolution fusion | flops 151093248 | bytes 4964356 | tf_op jit(solution)/shard_map/while/body/eval_jaxpr/dot_general | solution.py:38
  40.4 6.2 %collective-permute-done = bf16[32,768]{1,0:T(8,128)(2,1)S(1)} collective-permute-done((bf16[32,768]{1,0:T(8,128)(2,1)S(1)}, bf16[32,768]{1,0:T(8,128)(2,1)S(1)}, u32[]{:S(2)}, u32[]{:S(2)}) %collective-permute-start) | collective-permute-done | bytes 49184 | tf_op jit(solution)/shard_map/while/body/eval_jaxpr/ppermute | solution.py:10
  47.2 3.8 %fusion.35 = bf16[512,3072]{1,0:T(8,128)(2,1)S(1)} fusion(bf16[512,3072]{1,0:T(8,128)(2,1)S(1)} %get-tuple-element.371, s32[]{:T(128)S(6)} %select_n.82, bf16[32,768]{1,0:T(8,128)(2,1)S(1)} %collective-permute-done, bf16[3072,768]{1,0:T(8,128)(2,1)} %get-tuple-element.385), kind=kOutput, calls=%fused_computation.1.clone.1 | convolution fusion | flops 151093248 | bytes 4964356 | tf_op jit(solution)/shard_map/while/body/eval_jaxpr/dot_general | solution.py:38
  51.1 6.2 %collective-permute-done = bf16[32,768]{1,0:T(8,128)(2,1)S(1)} collective-permute-done((bf16[32,768]{1,0:T(8,128)(2,1)S(1)}, bf16[32,768]{1,0:T(8,128)(2,1)S(1)}, u32[]{:S(2)}, u32[]{:S(2)}) %collective-permute-start) | collective-permute-done | bytes 49184 | tf_op jit(solution)/shard_map/while/body/eval_jaxpr/ppermute | solution.py:10
  57.9 3.8 %fusion.35 = bf16[512,3072]{1,0:T(8,128)(2,1)S(1)} fusion(bf16[512,3072]{1,0:T(8,128)(2,1)S(1)} %get-tuple-element.371, s32[]{:T(128)S(6)} %select_n.82, bf16[32,768]{1,0:T(8,128)(2,1)S(1)} %collective-permute-done, bf16[3072,768]{1,0:T(8,128)(2,1)} %get-tuple-element.385), kind=kOutput, calls=%fused_computation.1.clone.1 | convolution fusion | flops 151093248 | bytes 4964356 | tf_op jit(solution)/shard_map/while/body/eval_jaxpr/dot_general | solution.py:38
  61.8 6.2 %collective-permute-done = bf16[32,768]{1,0:T(8,128)(2,1)S(1)} collective-permute-done((bf16[32,768]{1,0:T(8,128)(2,1)S(1)}, bf16[32,768]{1,0:T(8,128)(2,1)S(1)}, u32[]{:S(2)}, u32[]{:S(2)}) %collective-permute-start) | collective-permute-done | bytes 49184 | tf_op jit(solution)/shard_map/while/body/eval_jaxpr/ppermute | solution.py:10
  68.6 3.8 %fusion.35 = bf16[512,3072]{1,0:T(8,128)(2,1)S(1)} fusion(bf16[512,3072]{1,0:T(8,128)(2,1)S(1)} %get-tuple-element.371, s32[]{:T(128)S(6)} %select_n.82, bf16[32,768]{1,0:T(8,128)(2,1)S(1)} %collective-permute-done, bf16[3072,768]{1,0:T(8,128)(2,1)} %get-tuple-element.385), kind=kOutput, calls=%fused_computation.1.clone.1 | convolution fusion | flops 151093248 | bytes 4964356 | tf_op jit(solution)/shard_map/while/body/eval_jaxpr/dot_general | solution.py:38
  72.5 6.2 %collective-permute-done = bf16[32,768]{1,0:T(8,128)(2,1)S(1)} collective-permute-done((bf16[32,768]{1,0:T(8,128)(2,1)S(1)}, bf16[32,768]{1,0:T(8,128)(2,1)S(1)}, u32[]{:S(2)}, u32[]{:S(2)}) %collective-permute-start) | collective-permute-done | bytes 49184 | tf_op jit(solution)/shard_map/while/body/eval_jaxpr/ppermute | solution.py:10
  79.2 3.8 %fusion.35 = bf16[512,3072]{1,0:T(8,128)(2,1)S(1)} fusion(bf16[512,3072]{1,0:T(8,128)(2,1)S(1)} %get-tuple-element.371, s32[]{:T(128)S(6)} %select_n.82, bf16[32,768]{1,0:T(8,128)(2,1)S(1)} %collective-permute-done, bf16[3072,768]{1,0:T(8,128)(2,1)} %get-tuple-element.385), kind=kOutput, calls=%fused_computation.1.clone.1 | convolution fusion | flops 151093248 | bytes 4964356 | tf_op jit(solution)/shard_map/while/body/eval_jaxpr/dot_general | solution.py:38
  83.1 6.2 %collective-permute-done = bf16[32,768]{1,0:T(8,128)(2,1)S(1)} collective-permute-done((bf16[32,768]{1,0:T(8,128)(2,1)S(1)}, bf16[32,768]{1,0:T(8,128)(2,1)S(1)}, u32[]{:S(2)}, u32[]{:S(2)}) %collective-permute-start) | collective-permute-done | bytes 49184 | tf_op jit(solution)/shard_map/while/body/eval_jaxpr/ppermute | solution.py:10
  89.9 3.8 %fusion.35 = bf16[512,3072]{1,0:T(8,128)(2,1)S(1)} fusion(bf16[512,3072]{1,0:T(8,128)(2,1)S(1)} %get-tuple-element.371, s32[]{:T(128)S(6)} %select_n.82, bf16[32,768]{1,0:T(8,128)(2,1)S(1)} %collective-permute-done, bf16[3072,768]{1,0:T(8,128)(2,1)} %get-tuple-element.385), kind=kOutput, calls=%fused_computation.1.clone.1 | convolution fusion | flops 151093248 | bytes 4964356 | tf_op jit(solution)/shard_map/while/body/eval_jaxpr/dot_general | solution.py:38
  93.8 6.2 %collective-permute-done = bf16[32,768]{1,0:T(8,128)(2,1)S(1)} collective-permute-done((bf16[32,768]{1,0:T(8,128)(2,1)S(1)}, bf16[32,768]{1,0:T(8,128)(2,1)S(1)}, u32[]{:S(2)}, u32[]{:S(2)}) %collective-permute-start) | collective-permute-done | bytes 49184 | tf_op jit(solution)/shard_map/while/body/eval_jaxpr/ppermute | solution.py:10
  100.6 3.8 %fusion.35 = bf16[512,3072]{1,0:T(8,128)(2,1)S(1)} fusion(bf16[512,3072]{1,0:T(8,128)(2,1)S(1)} %get-tuple-element.371, s32[]{:T(128)S(6)} %select_n.82, bf16[32,768]{1,0:T(8,128)(2,1)S(1)} %collective-permute-done, bf16[3072,768]{1,0:T(8,128)(2,1)} %get-tuple-element.385), kind=kOutput, calls=%fused_computation.1.clone.1 | convolution fusion | flops 151093248 | bytes 4964356 | tf_op jit(solution)/shard_map/while/body/eval_jaxpr/dot_general | solution.py:38
  104.5 6.2 %collective-permute-done = bf16[32,768]{1,0:T(8,128)(2,1)S(1)} collective-permute-done((bf16[32,768]{1,0:T(8,128)(2,1)S(1)}, bf16[32,768]{1,0:T(8,128)(2,1)S(1)}, u32[]{:S(2)}, u32[]{:S(2)}) %collective-permute-start) | collective-permute-done | bytes 49184 | tf_op jit(solution)/shard_map/while/body/eval_jaxpr/ppermute | solution.py:10
  111.3 3.8 %fusion.35 = bf16[512,3072]{1,0:T(8,128)(2,1)S(1)} fusion(bf16[512,3072]{1,0:T(8,128)(2,1)S(1)} %get-tuple-element.371, s32[]{:T(128)S(6)} %select_n.82, bf16[32,768]{1,0:T(8,128)(2,1)S(1)} %collective-permute-done, bf16[3072,768]{1,0:T(8,128)(2,1)} %get-tuple-element.385), kind=kOutput, calls=%fused_computation.1.clone.1 | convolution fusion | flops 151093248 | bytes 4964356 | tf_op jit(solution)/shard_map/while/body/eval_jaxpr/dot_general | solution.py:38
  115.2 6.2 %collective-permute-done = bf16[32,768]{1,0:T(8,128)(2,1)S(1)} collective-permute-done((bf16[32,768]{1,0:T(8,128)(2,1)S(1)}, bf16[32,768]{1,0:T(8,128)(2,1)S(1)}, u32[]{:S(2)}, u32[]{:S(2)}) %collective-permute-start) | collective-permute-done | bytes 49184 | tf_op jit(solution)/shard_map/while/body/eval_jaxpr/ppermute | solution.py:10
  122.0 3.8 %fusion.35 = bf16[512,3072]{1,0:T(8,128)(2,1)S(1)} fusion(bf16[512,3072]{1,0:T(8,128)(2,1)S(1)} %get-tuple-element.371, s32[]{:T(128)S(6)} %select_n.82, bf16[32,768]{1,0:T(8,128)(2,1)S(1)} %collective-permute-done, bf16[3072,768]{1,0:T(8,128)(2,1)} %get-tuple-element.385), kind=kOutput, calls=%fused_computation.1.clone.1 | convolution fusion | flops 151093248 | bytes 4964356 | tf_op jit(solution)/shard_map/while/body/eval_jaxpr/dot_general | solution.py:38
  125.9 6.2 %collective-permute-done = bf16[32,768]{1,0:T(8,128)(2,1)S(1)} collective-permute-done((bf16[32,768]{1,0:T(8,128)(2,1)S(1)}, bf16[32,768]{1,0:T(8,128)(2,1)S(1)}, u32[]{:S(2)}, u32[]{:S(2)}) %collective-permute-start) | collective-permute-done | bytes 49184 | tf_op jit(solution)/shard_map/while/body/eval_jaxpr/ppermute | solution.py:10
  132.7 3.8 %fusion.35 = bf16[512,3072]{1,0:T(8,128)(2,1)S(1)} fusion(bf16[512,3072]{1,0:T(8,128)(2,1)S(1)} %get-tuple-element.371, s32[]{:T(128)S(6)} %select_n.82, bf16[32,768]{1,0:T(8,128)(2,1)S(1)} %collective-permute-done, bf16[3072,768]{1,0:T(8,128)(2,1)} %get-tuple-element.385), kind=kOutput, calls=%fused_computation.1.clone.1 | convolution fusion | flops 151093248 | bytes 4964356 | tf_op jit(solution)/shard_map/while/body/eval_jaxpr/dot_general | solution.py:38
  136.6 6.2 %collective-permute-done = bf16[32,768]{1,0:T(8,128)(2,1)S(1)} collective-permute-done((bf16[32,768]{1,0:T(8,128)(2,1)S(1)}, bf16[32,768]{1,0:T(8,128)(2,1)S(1)}, u32[]{:S(2)}, u32[]{:S(2)}) %collective-permute-start) | collective-permute-done | bytes 49184 | tf_op jit(solution)/shard_map/while/body/eval_jaxpr/ppermute | solution.py:10
  143.4 3.8 %fusion.35 = bf16[512,3072]{1,0:T(8,128)(2,1)S(1)} fusion(bf16[512,3072]{1,0:T(8,128)(2,1)S(1)} %get-tuple-element.371, s32[]{:T(128)S(6)} %select_n.82, bf16[32,768]{1,0:T(8,128)(2,1)S(1)} %collective-permute-done, bf16[3072,768]{1,0:T(8,128)(2,1)} %get-tuple-element.385), kind=kOutput, calls=%fused_computation.1.clone.1 | convolution fusion | flops 151093248 | bytes 4964356 | tf_op jit(solution)/shard_map/while/body/eval_jaxpr/dot_general | solution.py:38
  147.3 6.2 %collective-permute-done = bf16[32,768]{1,0:T(8,128)(2,1)S(1)} collective-permute-done((bf16[32,768]{1,0:T(8,128)(2,1)S(1)}, bf16[32,768]{1,0:T(8,128)(2,1)S(1)}, u32[]{:S(2)}, u32[]{:S(2)}) %collective-permute-start) | collective-permute-done | bytes 49184 | tf_op jit(solution)/shard_map/while/body/eval_jaxpr/ppermute | solution.py:10
  154.1 3.8 %fusion.35 = bf16[512,3072]{1,0:T(8,128)(2,1)S(1)} fusion(bf16[512,3072]{1,0:T(8,128)(2,1)S(1)} %get-tuple-element.371, s32[]{:T(128)S(6)} %select_n.82, bf16[32,768]{1,0:T(8,128)(2,1)S(1)} %collective-permute-done, bf16[3072,768]{1,0:T(8,128)(2,1)} %get-tuple-element.385), kind=kOutput, calls=%fused_computation.1.clone.1 | convolution fusion | flops 151093248 | bytes 4964356 | tf_op jit(solution)/shard_map/while/body/eval_jaxpr/dot_general | solution.py:38
  158.0 6.2 %collective-permute-done = bf16[32,768]{1,0:T(8,128)(2,1)S(1)} collective-permute-done((bf16[32,768]{1,0:T(8,128)(2,1)S(1)}, bf16[32,768]{1,0:T(8,128)(2,1)S(1)}, u32[]{:S(2)}, u32[]{:S(2)}) %collective-permute-start) | collective-permute-done | bytes 49184 | tf_op jit(solution)/shard_map/while/body/eval_jaxpr/ppermute | solution.py:10
  164.8 3.8 %fusion.35 = bf16[512,3072]{1,0:T(8,128)(2,1)S(1)} fusion(bf16[512,3072]{1,0:T(8,128)(2,1)S(1)} %get-tuple-element.371, s32[]{:T(128)S(6)} %select_n.82, bf16[32,768]{1,0:T(8,128)(2,1)S(1)} %collective-permute-done, bf16[3072,768]{1,0:T(8,128)(2,1)} %get-tuple-element.385), kind=kOutput, calls=%fused_computation.1.clone.1 | convolution fusion | flops 151093248 | bytes 4964356 | tf_op jit(solution)/shard_map/while/body/eval_jaxpr/dot_general | solution.py:38
  168.6 169.2 %while.35 = (s32[]{:T(128)}, f32[32,3072]{1,0:T(8,128)S(1)}, s32[]{:T(128)}, bf16[16,32,3072]{2,1,0:T(8,128)(2,1)S(1)}, s32[]{:T(128)}, /*index=5*/s32[]{:T(128)}, s32[]{:T(128)}, s32[]{:T(128)}) while((s32[]{:T(128)}, f32[32,3072]{1,0:T(8,128)S(1)}, s32[]{:T(128)}, bf16[16,32,3072]{2,1,0:T(8,128)(2,1)S(1)}, s32[]{:T(128)}, ...), condition=%wide.region_3.4_spmd, body=%wide.region_2.3_spmd.sunk | while | flops 393233 | bytes 2949432 | solution.py:79
  169.3 8.9 %collective-permute-done.1 = bf16[32,3072]{1,0:T(8,128)(2,1)S(1)} collective-permute-done((bf16[32,3072]{1,0:T(8,128)(2,1)}, bf16[32,3072]{1,0:T(8,128)(2,1)S(1)}, u32[]{:S(2)}, u32[]{:S(2)}) %collective-permute-start.1) | collective-permute-done | bytes 196640 | tf_op jit(solution)/shard_map/while/body/eval_jaxpr/ppermute | solution.py:10
  180.6 8.9 %collective-permute-done.1 = bf16[32,3072]{1,0:T(8,128)(2,1)S(1)} collective-permute-done((bf16[32,3072]{1,0:T(8,128)(2,1)}, bf16[32,3072]{1,0:T(8,128)(2,1)S(1)}, u32[]{:S(2)}, u32[]{:S(2)}) %collective-permute-start.1) | collective-permute-done | bytes 196640 | tf_op jit(solution)/shard_map/while/body/eval_jaxpr/ppermute | solution.py:10
  191.9 8.9 %collective-permute-done.1 = bf16[32,3072]{1,0:T(8,128)(2,1)S(1)} collective-permute-done((bf16[32,3072]{1,0:T(8,128)(2,1)}, bf16[32,3072]{1,0:T(8,128)(2,1)S(1)}, u32[]{:S(2)}, u32[]{:S(2)}) %collective-permute-start.1) | collective-permute-done | bytes 196640 | tf_op jit(solution)/shard_map/while/body/eval_jaxpr/ppermute | solution.py:10
  203.2 8.9 %collective-permute-done.1 = bf16[32,3072]{1,0:T(8,128)(2,1)S(1)} collective-permute-done((bf16[32,3072]{1,0:T(8,128)(2,1)}, bf16[32,3072]{1,0:T(8,128)(2,1)S(1)}, u32[]{:S(2)}, u32[]{:S(2)}) %collective-permute-start.1) | collective-permute-done | bytes 196640 | tf_op jit(solution)/shard_map/while/body/eval_jaxpr/ppermute | solution.py:10
  214.5 8.9 %collective-permute-done.1 = bf16[32,3072]{1,0:T(8,128)(2,1)S(1)} collective-permute-done((bf16[32,3072]{1,0:T(8,128)(2,1)}, bf16[32,3072]{1,0:T(8,128)(2,1)S(1)}, u32[]{:S(2)}, u32[]{:S(2)}) %collective-permute-start.1) | collective-permute-done | bytes 196640 | tf_op jit(solution)/shard_map/while/body/eval_jaxpr/ppermute | solution.py:10
  225.8 8.9 %collective-permute-done.1 = bf16[32,3072]{1,0:T(8,128)(2,1)S(1)} collective-permute-done((bf16[32,3072]{1,0:T(8,128)(2,1)}, bf16[32,3072]{1,0:T(8,128)(2,1)S(1)}, u32[]{:S(2)}, u32[]{:S(2)}) %collective-permute-start.1) | collective-permute-done | bytes 196640 | tf_op jit(solution)/shard_map/while/body/eval_jaxpr/ppermute | solution.py:10
  237.0 8.9 %collective-permute-done.1 = bf16[32,3072]{1,0:T(8,128)(2,1)S(1)} collective-permute-done((bf16[32,3072]{1,0:T(8,128)(2,1)}, bf16[32,3072]{1,0:T(8,128)(2,1)S(1)}, u32[]{:S(2)}, u32[]{:S(2)}) %collective-permute-start.1) | collective-permute-done | bytes 196640 | tf_op jit(solution)/shard_map/while/body/eval_jaxpr/ppermute | solution.py:10
  248.3 8.9 %collective-permute-done.1 = bf16[32,3072]{1,0:T(8,128)(2,1)S(1)} collective-permute-done((bf16[32,3072]{1,0:T(8,128)(2,1)}, bf16[32,3072]{1,0:T(8,128)(2,1)S(1)}, u32[]{:S(2)}, u32[]{:S(2)}) %collective-permute-start.1) | collective-permute-done | bytes 196640 | tf_op jit(solution)/shard_map/while/body/eval_jaxpr/ppermute | solution.py:10
  259.6 8.9 %collective-permute-done.1 = bf16[32,3072]{1,0:T(8,128)(2,1)S(1)} collective-permute-done((bf16[32,3072]{1,0:T(8,128)(2,1)}, bf16[32,3072]{1,0:T(8,128)(2,1)S(1)}, u32[]{:S(2)}, u32[]{:S(2)}) %collective-permute-start.1) | collective-permute-done | bytes 196640 | tf_op jit(solution)/shard_map/while/body/eval_jaxpr/ppermute | solution.py:10
  270.9 8.9 %collective-permute-done.1 = bf16[32,3072]{1,0:T(8,128)(2,1)S(1)} collective-permute-done((bf16[32,3072]{1,0:T(8,128)(2,1)}, bf16[32,3072]{1,0:T(8,128)(2,1)S(1)}, u32[]{:S(2)}, u32[]{:S(2)}) %collective-permute-start.1) | collective-permute-done | bytes 196640 | tf_op jit(solution)/shard_map/while/body/eval_jaxpr/ppermute | solution.py:10
  282.2 8.9 %collective-permute-done.1 = bf16[32,3072]{1,0:T(8,128)(2,1)S(1)} collective-permute-done((bf16[32,3072]{1,0:T(8,128)(2,1)}, bf16[32,3072]{1,0:T(8,128)(2,1)S(1)}, u32[]{:S(2)}, u32[]{:S(2)}) %collective-permute-start.1) | collective-permute-done | bytes 196640 | tf_op jit(solution)/shard_map/while/body/eval_jaxpr/ppermute | solution.py:10
  293.4 8.9 %collective-permute-done.1 = bf16[32,3072]{1,0:T(8,128)(2,1)S(1)} collective-permute-done((bf16[32,3072]{1,0:T(8,128)(2,1)}, bf16[32,3072]{1,0:T(8,128)(2,1)S(1)}, u32[]{:S(2)}, u32[]{:S(2)}) %collective-permute-start.1) | collective-permute-done | bytes 196640 | tf_op jit(solution)/shard_map/while/body/eval_jaxpr/ppermute | solution.py:10
  304.7 8.9 %collective-permute-done.1 = bf16[32,3072]{1,0:T(8,128)(2,1)S(1)} collective-permute-done((bf16[32,3072]{1,0:T(8,128)(2,1)}, bf16[32,3072]{1,0:T(8,128)(2,1)S(1)}, u32[]{:S(2)}, u32[]{:S(2)}) %collective-permute-start.1) | collective-permute-done | bytes 196640 | tf_op jit(solution)/shard_map/while/body/eval_jaxpr/ppermute | solution.py:10
  316.0 8.9 %collective-permute-done.1 = bf16[32,3072]{1,0:T(8,128)(2,1)S(1)} collective-permute-done((bf16[32,3072]{1,0:T(8,128)(2,1)}, bf16[32,3072]{1,0:T(8,128)(2,1)S(1)}, u32[]{:S(2)}, u32[]{:S(2)}) %collective-permute-start.1) | collective-permute-done | bytes 196640 | tf_op jit(solution)/shard_map/while/body/eval_jaxpr/ppermute | solution.py:10
  327.3 8.9 %collective-permute-done.1 = bf16[32,3072]{1,0:T(8,128)(2,1)S(1)} collective-permute-done((bf16[32,3072]{1,0:T(8,128)(2,1)}, bf16[32,3072]{1,0:T(8,128)(2,1)S(1)}, u32[]{:S(2)}, u32[]{:S(2)}) %collective-permute-start.1) | collective-permute-done | bytes 196640 | tf_op jit(solution)/shard_map/while/body/eval_jaxpr/ppermute | solution.py:10
  339.7 8.0 %convolution_convert_fusion.1 = bf16[3072,768]{1,0:T(8,128)(2,1)} fusion(bf16[512,768]{1,0:T(8,128)(2,1)} %get-tuple-element.274, bf16[512,3072]{1,0:T(8,128)(2,1)} %param.8), kind=kOutput, calls=%fused_computation.14 | convolution fusion | flops 2434007040 | bytes 8650752 | tf_op jit(solution)/shard_map/dot_general | solution.py:63
  (129 shorter events, 55.4 us)
Async XLA Ops:
  5.7 0.9 copy-start.1
  6.6 7.9 %collective-permute-start = (bf16[32,768]{1,0:T(8,128)(2,1)S(1)}, bf16[32,768]{1,0:T(8,128)(2,1)S(1)}, u32[]{:S(2)}, u32[]{:S(2)}) collective-permute-start(bf16[32,768]{1,0:T(8,128)(2,1)S(1)} %get-tuple-element.370), channel_id=1, source_target_pairs={{240,0},{0,16},{16,32},{32,48},{48,64},{64,80},{80,96},{96,112},{1... | collective-permute-start | bytes 147464 | tf_op jit(solution)/shard_map/while/body/eval_jaxpr/ppermute | solution.py:10
  18.9 6.3 %collective-permute-start = (bf16[32,768]{1,0:T(8,128)(2,1)S(1)}, bf16[32,768]{1,0:T(8,128)(2,1)S(1)}, u32[]{:S(2)}, u32[]{:S(2)}) collective-permute-start(bf16[32,768]{1,0:T(8,128)(2,1)S(1)} %get-tuple-element.370), channel_id=1, source_target_pairs={{240,0},{0,16},{16,32},{32,48},{48,64},{64,80},{80,96},{96,112},{1... | collective-permute-start | bytes 147464 | tf_op jit(solution)/shard_map/while/body/eval_jaxpr/ppermute | solution.py:10
  29.6 6.3 %collective-permute-start = (bf16[32,768]{1,0:T(8,128)(2,1)S(1)}, bf16[32,768]{1,0:T(8,128)(2,1)S(1)}, u32[]{:S(2)}, u32[]{:S(2)}) collective-permute-start(bf16[32,768]{1,0:T(8,128)(2,1)S(1)} %get-tuple-element.370), channel_id=1, source_target_pairs={{240,0},{0,16},{16,32},{32,48},{48,64},{64,80},{80,96},{96,112},{1... | collective-permute-start | bytes 147464 | tf_op jit(solution)/shard_map/while/body/eval_jaxpr/ppermute | solution.py:10
  40.3 6.3 %collective-permute-start = (bf16[32,768]{1,0:T(8,128)(2,1)S(1)}, bf16[32,768]{1,0:T(8,128)(2,1)S(1)}, u32[]{:S(2)}, u32[]{:S(2)}) collective-permute-start(bf16[32,768]{1,0:T(8,128)(2,1)S(1)} %get-tuple-element.370), channel_id=1, source_target_pairs={{240,0},{0,16},{16,32},{32,48},{48,64},{64,80},{80,96},{96,112},{1... | collective-permute-start | bytes 147464 | tf_op jit(solution)/shard_map/while/body/eval_jaxpr/ppermute | solution.py:10
  51.0 6.3 %collective-permute-start = (bf16[32,768]{1,0:T(8,128)(2,1)S(1)}, bf16[32,768]{1,0:T(8,128)(2,1)S(1)}, u32[]{:S(2)}, u32[]{:S(2)}) collective-permute-start(bf16[32,768]{1,0:T(8,128)(2,1)S(1)} %get-tuple-element.370), channel_id=1, source_target_pairs={{240,0},{0,16},{16,32},{32,48},{48,64},{64,80},{80,96},{96,112},{1... | collective-permute-start | bytes 147464 | tf_op jit(solution)/shard_map/while/body/eval_jaxpr/ppermute | solution.py:10
  61.7 6.3 %collective-permute-start = (bf16[32,768]{1,0:T(8,128)(2,1)S(1)}, bf16[32,768]{1,0:T(8,128)(2,1)S(1)}, u32[]{:S(2)}, u32[]{:S(2)}) collective-permute-start(bf16[32,768]{1,0:T(8,128)(2,1)S(1)} %get-tuple-element.370), channel_id=1, source_target_pairs={{240,0},{0,16},{16,32},{32,48},{48,64},{64,80},{80,96},{96,112},{1... | collective-permute-start | bytes 147464 | tf_op jit(solution)/shard_map/while/body/eval_jaxpr/ppermute | solution.py:10
  72.3 6.3 %collective-permute-start = (bf16[32,768]{1,0:T(8,128)(2,1)S(1)}, bf16[32,768]{1,0:T(8,128)(2,1)S(1)}, u32[]{:S(2)}, u32[]{:S(2)}) collective-permute-start(bf16[32,768]{1,0:T(8,128)(2,1)S(1)} %get-tuple-element.370), channel_id=1, source_target_pairs={{240,0},{0,16},{16,32},{32,48},{48,64},{64,80},{80,96},{96,112},{1... | collective-permute-start | bytes 147464 | tf_op jit(solution)/shard_map/while/body/eval_jaxpr/ppermute | solution.py:10
  83.0 6.3 %collective-permute-start = (bf16[32,768]{1,0:T(8,128)(2,1)S(1)}, bf16[32,768]{1,0:T(8,128)(2,1)S(1)}, u32[]{:S(2)}, u32[]{:S(2)}) collective-permute-start(bf16[32,768]{1,0:T(8,128)(2,1)S(1)} %get-tuple-element.370), channel_id=1, source_target_pairs={{240,0},{0,16},{16,32},{32,48},{48,64},{64,80},{80,96},{96,112},{1... | collective-permute-start | bytes 147464 | tf_op jit(solution)/shard_map/while/body/eval_jaxpr/ppermute | solution.py:10
  93.7 6.3 %collective-permute-start = (bf16[32,768]{1,0:T(8,128)(2,1)S(1)}, bf16[32,768]{1,0:T(8,128)(2,1)S(1)}, u32[]{:S(2)}, u32[]{:S(2)}) collective-permute-start(bf16[32,768]{1,0:T(8,128)(2,1)S(1)} %get-tuple-element.370), channel_id=1, source_target_pairs={{240,0},{0,16},{16,32},{32,48},{48,64},{64,80},{80,96},{96,112},{1... | collective-permute-start | bytes 147464 | tf_op jit(solution)/shard_map/while/body/eval_jaxpr/ppermute | solution.py:10
  104.4 6.3 %collective-permute-start = (bf16[32,768]{1,0:T(8,128)(2,1)S(1)}, bf16[32,768]{1,0:T(8,128)(2,1)S(1)}, u32[]{:S(2)}, u32[]{:S(2)}) collective-permute-start(bf16[32,768]{1,0:T(8,128)(2,1)S(1)} %get-tuple-element.370), channel_id=1, source_target_pairs={{240,0},{0,16},{16,32},{32,48},{48,64},{64,80},{80,96},{96,112},{1... | collective-permute-start | bytes 147464 | tf_op jit(solution)/shard_map/while/body/eval_jaxpr/ppermute | solution.py:10
  115.1 6.3 %collective-permute-start = (bf16[32,768]{1,0:T(8,128)(2,1)S(1)}, bf16[32,768]{1,0:T(8,128)(2,1)S(1)}, u32[]{:S(2)}, u32[]{:S(2)}) collective-permute-start(bf16[32,768]{1,0:T(8,128)(2,1)S(1)} %get-tuple-element.370), channel_id=1, source_target_pairs={{240,0},{0,16},{16,32},{32,48},{48,64},{64,80},{80,96},{96,112},{1... | collective-permute-start | bytes 147464 | tf_op jit(solution)/shard_map/while/body/eval_jaxpr/ppermute | solution.py:10
  125.8 6.3 %collective-permute-start = (bf16[32,768]{1,0:T(8,128)(2,1)S(1)}, bf16[32,768]{1,0:T(8,128)(2,1)S(1)}, u32[]{:S(2)}, u32[]{:S(2)}) collective-permute-start(bf16[32,768]{1,0:T(8,128)(2,1)S(1)} %get-tuple-element.370), channel_id=1, source_target_pairs={{240,0},{0,16},{16,32},{32,48},{48,64},{64,80},{80,96},{96,112},{1... | collective-permute-start | bytes 147464 | tf_op jit(solution)/shard_map/while/body/eval_jaxpr/ppermute | solution.py:10
  136.5 6.3 %collective-permute-start = (bf16[32,768]{1,0:T(8,128)(2,1)S(1)}, bf16[32,768]{1,0:T(8,128)(2,1)S(1)}, u32[]{:S(2)}, u32[]{:S(2)}) collective-permute-start(bf16[32,768]{1,0:T(8,128)(2,1)S(1)} %get-tuple-element.370), channel_id=1, source_target_pairs={{240,0},{0,16},{16,32},{32,48},{48,64},{64,80},{80,96},{96,112},{1... | collective-permute-start | bytes 147464 | tf_op jit(solution)/shard_map/while/body/eval_jaxpr/ppermute | solution.py:10
  147.2 6.3 %collective-permute-start = (bf16[32,768]{1,0:T(8,128)(2,1)S(1)}, bf16[32,768]{1,0:T(8,128)(2,1)S(1)}, u32[]{:S(2)}, u32[]{:S(2)}) collective-permute-start(bf16[32,768]{1,0:T(8,128)(2,1)S(1)} %get-tuple-element.370), channel_id=1, source_target_pairs={{240,0},{0,16},{16,32},{32,48},{48,64},{64,80},{80,96},{96,112},{1... | collective-permute-start | bytes 147464 | tf_op jit(solution)/shard_map/while/body/eval_jaxpr/ppermute | solution.py:10
  157.9 6.3 %collective-permute-start = (bf16[32,768]{1,0:T(8,128)(2,1)S(1)}, bf16[32,768]{1,0:T(8,128)(2,1)S(1)}, u32[]{:S(2)}, u32[]{:S(2)}) collective-permute-start(bf16[32,768]{1,0:T(8,128)(2,1)S(1)} %get-tuple-element.370), channel_id=1, source_target_pairs={{240,0},{0,16},{16,32},{32,48},{48,64},{64,80},{80,96},{96,112},{1... | collective-permute-start | bytes 147464 | tf_op jit(solution)/shard_map/while/body/eval_jaxpr/ppermute | solution.py:10
  169.3 8.9 %collective-permute-start.1 = (bf16[32,3072]{1,0:T(8,128)(2,1)}, bf16[32,3072]{1,0:T(8,128)(2,1)S(1)}, u32[]{:S(2)}, u32[]{:S(2)}) collective-permute-start(bf16[32,3072]{1,0:T(8,128)(2,1)} %convert_element_type.154), channel_id=1, source_target_pairs={{15,0},{0,1},{1,2},{2,3},{3,4},{4,5},{5,6},{6,7},{7,8},{8,9},{9,10... | collective-permute-start | bytes 589832 | tf_op jit(solution)/shard_map/while/body/eval_jaxpr/ppermute | solution.py:10
  178.3 0.7 copy-start
  180.6 8.9 %collective-permute-start.1 = (bf16[32,3072]{1,0:T(8,128)(2,1)}, bf16[32,3072]{1,0:T(8,128)(2,1)S(1)}, u32[]{:S(2)}, u32[]{:S(2)}) collective-permute-start(bf16[32,3072]{1,0:T(8,128)(2,1)} %convert_element_type.154), channel_id=1, source_target_pairs={{15,0},{0,1},{1,2},{2,3},{3,4},{4,5},{5,6},{6,7},{7,8},{8,9},{9,10... | collective-permute-start | bytes 589832 | tf_op jit(solution)/shard_map/while/body/eval_jaxpr/ppermute | solution.py:10
  189.5 0.7 copy-start
  191.9 8.9 %collective-permute-start.1 = (bf16[32,3072]{1,0:T(8,128)(2,1)}, bf16[32,3072]{1,0:T(8,128)(2,1)S(1)}, u32[]{:S(2)}, u32[]{:S(2)}) collective-permute-start(bf16[32,3072]{1,0:T(8,128)(2,1)} %convert_element_type.154), channel_id=1, source_target_pairs={{15,0},{0,1},{1,2},{2,3},{3,4},{4,5},{5,6},{6,7},{7,8},{8,9},{9,10... | collective-permute-start | bytes 589832 | tf_op jit(solution)/shard_map/while/body/eval_jaxpr/ppermute | solution.py:10
  200.8 0.7 copy-start
  203.2 8.9 %collective-permute-start.1 = (bf16[32,3072]{1,0:T(8,128)(2,1)}, bf16[32,3072]{1,0:T(8,128)(2,1)S(1)}, u32[]{:S(2)}, u32[]{:S(2)}) collective-permute-start(bf16[32,3072]{1,0:T(8,128)(2,1)} %convert_element_type.154), channel_id=1, source_target_pairs={{15,0},{0,1},{1,2},{2,3},{3,4},{4,5},{5,6},{6,7},{7,8},{8,9},{9,10... | collective-permute-start | bytes 589832 | tf_op jit(solution)/shard_map/while/body/eval_jaxpr/ppermute | solution.py:10
  212.1 0.7 copy-start
  214.5 8.9 %collective-permute-start.1 = (bf16[32,3072]{1,0:T(8,128)(2,1)}, bf16[32,3072]{1,0:T(8,128)(2,1)S(1)}, u32[]{:S(2)}, u32[]{:S(2)}) collective-permute-start(bf16[32,3072]{1,0:T(8,128)(2,1)} %convert_element_type.154), channel_id=1, source_target_pairs={{15,0},{0,1},{1,2},{2,3},{3,4},{4,5},{5,6},{6,7},{7,8},{8,9},{9,10... | collective-permute-start | bytes 589832 | tf_op jit(solution)/shard_map/while/body/eval_jaxpr/ppermute | solution.py:10
  223.4 0.7 copy-start
  225.8 8.9 %collective-permute-start.1 = (bf16[32,3072]{1,0:T(8,128)(2,1)}, bf16[32,3072]{1,0:T(8,128)(2,1)S(1)}, u32[]{:S(2)}, u32[]{:S(2)}) collective-permute-start(bf16[32,3072]{1,0:T(8,128)(2,1)} %convert_element_type.154), channel_id=1, source_target_pairs={{15,0},{0,1},{1,2},{2,3},{3,4},{4,5},{5,6},{6,7},{7,8},{8,9},{9,10... | collective-permute-start | bytes 589832 | tf_op jit(solution)/shard_map/while/body/eval_jaxpr/ppermute | solution.py:10
  234.7 0.7 copy-start
  237.0 8.9 %collective-permute-start.1 = (bf16[32,3072]{1,0:T(8,128)(2,1)}, bf16[32,3072]{1,0:T(8,128)(2,1)S(1)}, u32[]{:S(2)}, u32[]{:S(2)}) collective-permute-start(bf16[32,3072]{1,0:T(8,128)(2,1)} %convert_element_type.154), channel_id=1, source_target_pairs={{15,0},{0,1},{1,2},{2,3},{3,4},{4,5},{5,6},{6,7},{7,8},{8,9},{9,10... | collective-permute-start | bytes 589832 | tf_op jit(solution)/shard_map/while/body/eval_jaxpr/ppermute | solution.py:10
  246.0 0.7 copy-start
  248.3 8.9 %collective-permute-start.1 = (bf16[32,3072]{1,0:T(8,128)(2,1)}, bf16[32,3072]{1,0:T(8,128)(2,1)S(1)}, u32[]{:S(2)}, u32[]{:S(2)}) collective-permute-start(bf16[32,3072]{1,0:T(8,128)(2,1)} %convert_element_type.154), channel_id=1, source_target_pairs={{15,0},{0,1},{1,2},{2,3},{3,4},{4,5},{5,6},{6,7},{7,8},{8,9},{9,10... | collective-permute-start | bytes 589832 | tf_op jit(solution)/shard_map/while/body/eval_jaxpr/ppermute | solution.py:10
  257.2 0.7 copy-start
  259.6 8.9 %collective-permute-start.1 = (bf16[32,3072]{1,0:T(8,128)(2,1)}, bf16[32,3072]{1,0:T(8,128)(2,1)S(1)}, u32[]{:S(2)}, u32[]{:S(2)}) collective-permute-start(bf16[32,3072]{1,0:T(8,128)(2,1)} %convert_element_type.154), channel_id=1, source_target_pairs={{15,0},{0,1},{1,2},{2,3},{3,4},{4,5},{5,6},{6,7},{7,8},{8,9},{9,10... | collective-permute-start | bytes 589832 | tf_op jit(solution)/shard_map/while/body/eval_jaxpr/ppermute | solution.py:10
  268.5 0.7 copy-start
  270.9 8.9 %collective-permute-start.1 = (bf16[32,3072]{1,0:T(8,128)(2,1)}, bf16[32,3072]{1,0:T(8,128)(2,1)S(1)}, u32[]{:S(2)}, u32[]{:S(2)}) collective-permute-start(bf16[32,3072]{1,0:T(8,128)(2,1)} %convert_element_type.154), channel_id=1, source_target_pairs={{15,0},{0,1},{1,2},{2,3},{3,4},{4,5},{5,6},{6,7},{7,8},{8,9},{9,10... | collective-permute-start | bytes 589832 | tf_op jit(solution)/shard_map/while/body/eval_jaxpr/ppermute | solution.py:10
  279.8 0.7 copy-start
  282.2 8.9 %collective-permute-start.1 = (bf16[32,3072]{1,0:T(8,128)(2,1)}, bf16[32,3072]{1,0:T(8,128)(2,1)S(1)}, u32[]{:S(2)}, u32[]{:S(2)}) collective-permute-start(bf16[32,3072]{1,0:T(8,128)(2,1)} %convert_element_type.154), channel_id=1, source_target_pairs={{15,0},{0,1},{1,2},{2,3},{3,4},{4,5},{5,6},{6,7},{7,8},{8,9},{9,10... | collective-permute-start | bytes 589832 | tf_op jit(solution)/shard_map/while/body/eval_jaxpr/ppermute | solution.py:10
  291.1 0.7 copy-start
  293.4 8.9 %collective-permute-start.1 = (bf16[32,3072]{1,0:T(8,128)(2,1)}, bf16[32,3072]{1,0:T(8,128)(2,1)S(1)}, u32[]{:S(2)}, u32[]{:S(2)}) collective-permute-start(bf16[32,3072]{1,0:T(8,128)(2,1)} %convert_element_type.154), channel_id=1, source_target_pairs={{15,0},{0,1},{1,2},{2,3},{3,4},{4,5},{5,6},{6,7},{7,8},{8,9},{9,10... | collective-permute-start | bytes 589832 | tf_op jit(solution)/shard_map/while/body/eval_jaxpr/ppermute | solution.py:10
  302.4 0.7 copy-start
  304.7 8.9 %collective-permute-start.1 = (bf16[32,3072]{1,0:T(8,128)(2,1)}, bf16[32,3072]{1,0:T(8,128)(2,1)S(1)}, u32[]{:S(2)}, u32[]{:S(2)}) collective-permute-start(bf16[32,3072]{1,0:T(8,128)(2,1)} %convert_element_type.154), channel_id=1, source_target_pairs={{15,0},{0,1},{1,2},{2,3},{3,4},{4,5},{5,6},{6,7},{7,8},{8,9},{9,10... | collective-permute-start | bytes 589832 | tf_op jit(solution)/shard_map/while/body/eval_jaxpr/ppermute | solution.py:10
  313.6 0.7 copy-start
  316.0 8.9 %collective-permute-start.1 = (bf16[32,3072]{1,0:T(8,128)(2,1)}, bf16[32,3072]{1,0:T(8,128)(2,1)S(1)}, u32[]{:S(2)}, u32[]{:S(2)}) collective-permute-start(bf16[32,3072]{1,0:T(8,128)(2,1)} %convert_element_type.154), channel_id=1, source_target_pairs={{15,0},{0,1},{1,2},{2,3},{3,4},{4,5},{5,6},{6,7},{7,8},{8,9},{9,10... | collective-permute-start | bytes 589832 | tf_op jit(solution)/shard_map/while/body/eval_jaxpr/ppermute | solution.py:10
  324.9 0.7 copy-start
  327.3 8.9 %collective-permute-start.1 = (bf16[32,3072]{1,0:T(8,128)(2,1)}, bf16[32,3072]{1,0:T(8,128)(2,1)S(1)}, u32[]{:S(2)}, u32[]{:S(2)}) collective-permute-start(bf16[32,3072]{1,0:T(8,128)(2,1)} %convert_element_type.154), channel_id=1, source_target_pairs={{15,0},{0,1},{1,2},{2,3},{3,4},{4,5},{5,6},{6,7},{7,8},{8,9},{9,10... | collective-permute-start | bytes 589832 | tf_op jit(solution)/shard_map/while/body/eval_jaxpr/ppermute | solution.py:10
  336.2 0.7 copy-start
where the time goes:
time: 349 us; the launch traced here: 348 us
  waiting for transfers between devices  226 us (65%)
  matrix products  68.6 us (20%)
  other arithmetic  26.9 us (8%)
  local copies, waits for them, and re-layouts  21.6 us (6%)
    ppermute x30, waiting for transfers between devices, from_behind(): return lax.ppermute(block, axis, route)  226 us
    dot_general x16, matrix products, record(): lax.dot_general(current, weight, (((1,), (1,)), ((), ())), preferred_elem...  60.6 us
    add x15, other arithmetic, chain_step(): return arrived + local_tile.astype(jnp.float32)  14.5 us
    convert_element_type x15, other arithmetic, chain_step(): running.astype(jnp.bfloat16)  10.5 us
    while x45, local copies, waits for them, and re-layouts  10.2 us
    dynamic_update_slice x16, local copies, waits for them, and re-layouts, record(): collected = lax.dynamic_update_slice_in_dim(collected, current, offset, 0)  9.28 us
    dot_general x1, matrix products, body(): lax.dot_general(activation, collected, (((0,), (0,)), ((), ())), preferre...  7.98 us
  transfers between devices with their start and end apart: 30, of which 30 were waited for; matrix products, arithmetic and copies ran while one was open for 0% of the time, Pallas kernels for 0%

commit v1 on v0

v1 whole, which is shorter than its diff:
```python
import jax
import jax.numpy as jnp
from jax import lax
from jax.experimental import pallas as pl
from jax.experimental.pallas import tpu as pltpu
from jax.sharding import PartitionSpec as P

MESH = pl.DeviceIdType.MESH
ROWS = 32
WIDTH = 768
HIDDEN = 3072
TOKENS = 512
PIECE = 512
HALVES = 2
HALF = HIDDEN // HALVES

BATCHES = (
    ((0, 0), (1, 0), (0, 3), (0, 5)),
    ((0, 2), (0, 6), (1, 3), (1, 5)),
    ((1, 2), (1, 6), (0, 1), (0, 7)),
    ((0, 4), (1, 4), (1, 1), (1, 7)),
)
SLOTS = tuple(slot for batch in BATCHES for slot in batch)
INDEX = {slot: i for i, slot in enumerate(SLOTS)}
SEND_ORDER = (3, 5, 2, 6, 4, 1, 7)


def gelu_value(values):
    inner = 0.7978845608 * (values + 0.044715 * values * values * values)
    return 0.5 * values * (1.0 + jnp.tanh(inner))


def gelu_slope(values):
    inner = 0.7978845608 * (values + 0.044715 * values * values * values)
    tanh_value = jnp.tanh(inner)
    return 0.5 * (1.0 + tanh_value) + 0.5 * values * (
        1.0 - tanh_value * tanh_value
    ) * 0.7978845608 * (1.0 + 3.0 * 0.044715 * values * values)


def kernel(
    grad_out, pre_act, weight, grad_pre, grad_weight,
    pre, wide, tiles, act, partial, from_core, pair_sum, arrived,
    load_sem, tile_send, tile_recv, forward_send, core_send, core_recv, sum_send, sum_recv,
):
    row, col = lax.axis_index("row"), lax.axis_index("col")
    x_lo, z = row // 8, row % 8
    chip, core = col // 2, col % 2

    def at_z(distance):
        return x_lo * 8 + (z + distance) % 8

    def token_tile(slot):
        other, distance = slot
        return ((x_lo + other) % 2) * 8 + (z + distance) % 8

    def tile_rows(slot):
        return pl.ds(INDEX[slot] * ROWS, ROWS)

    partner_row = (row + 8) % 16
    partner_core = chip * 2 + 1 - core
    pair = (z + core) % 2

    own_load = pltpu.make_async_copy(grad_out, tiles.at[tile_rows((0, 0))], load_sem.at[0])
    own_load.start()
    pre_load = pltpu.make_async_copy(pre_act, pre, load_sem.at[1])
    pre_load.start()
    weight_load = pltpu.make_async_copy(weight, wide, load_sem.at[2])
    weight_load.start()

    barrier = pltpu.get_barrier_semaphore()
    for distance in SEND_ORDER:
        pl.semaphore_signal(barrier, inc=1, device_id=(at_z(distance), col), device_id_type=MESH)
    pl.semaphore_signal(barrier, inc=1, device_id=(partner_row, col), device_id_type=MESH)
    pl.semaphore_signal(barrier, inc=1, device_id=(row, partner_core), device_id_type=MESH)
    for step in range(1, 8):
        pl.semaphore_signal(
            barrier, inc=1, device_id=(row, ((chip + step) % 8) * 2 + core), device_id_type=MESH
        )
    own_load.wait()
    pl.semaphore_wait(barrier, 16)

    sends = []

    def send_tile(source_slot, landing_slot, send_sem, device_row):
        copy = pltpu.make_async_remote_copy(
            src_ref=tiles.at[tile_rows(source_slot)],
            dst_ref=tiles.at[tile_rows(landing_slot)],
            send_sem=send_sem,
            recv_sem=tile_recv.at[INDEX[landing_slot]],
            device_id=(device_row, col),
            device_id_type=MESH,
        )
        copy.start()
        sends.append(copy)

    send_tile((0, 0), (1, 0), forward_send.at[0], partner_row)
    for distance in SEND_ORDER:
        send_tile((0, 0), (0, (8 - distance) % 8), tile_send.at[distance], at_z(distance))

    def wait_tile(slot):
        pltpu.make_async_remote_copy(
            src_ref=tiles.at[tile_rows(slot)],
            dst_ref=tiles.at[tile_rows(slot)],
            send_sem=forward_send.at[0],
            recv_sem=tile_recv.at[INDEX[slot]],
            device_id=(partner_row, col),
            device_id_type=MESH,
        ).wait_recv()

    def take_and_forward(distance):
        wait_tile((0, distance))
        send_tile((0, distance), (1, distance), forward_send.at[distance], partner_row)

    def activate(slot):
        start = pl.multiple_of(token_tile(slot) * ROWS, ROWS)
        base = INDEX[slot] * ROWS

        def step(i, carry):
            offset = pl.multiple_of(i * 16, 16)
            values = pre[pl.ds(start + offset, 16), :].astype(jnp.float32)
            act[pl.ds(base + offset, 16), :] = gelu_value(values).astype(jnp.bfloat16)
            return carry

        lax.fori_loop(0, ROWS // 16, step, 0)

    def partial_half(batch, half):
        rows = pl.ds(batch * 4 * ROWS, 4 * ROWS)

        def step(i, carry):
            offset = pl.multiple_of(half * HALF + i * PIECE, PIECE)
            product = lax.dot_general(
                tiles[rows, :], wide[pl.ds(offset, PIECE), :], (((1,), (1,)), ((), ())),
                preferred_element_type=jnp.float32,
            )
            partial[rows, pl.ds(offset, PIECE)] = product.astype(jnp.bfloat16)
            return carry

        lax.fori_loop(0, HALF // PIECE, step, 0)

    def core_copy(batch, half):
        theirs = pl.multiple_of(batch * 4 * ROWS + (1 - pair) * 2 * ROWS, 2 * ROWS)
        columns = pl.ds(half * HALF, HALF)
        return pltpu.make_async_remote_copy(
            src_ref=partial.at[pl.ds(theirs, 2 * ROWS), columns],
            dst_ref=from_core.at[batch, :, columns],
            send_sem=core_send.at[batch, half],
            recv_sem=core_recv.at[batch, half],
            device_id=(row, partner_core),
            device_id_type=MESH,
        )

    def add_cores(batch, half):
        mine = pl.multiple_of(batch * 4 * ROWS + pair * 2 * ROWS, 2 * ROWS)
        columns = pl.ds(half * HALF, HALF)

        def step(i, carry):
            offset = pl.multiple_of(i * 16, 16)
            total = partial[pl.ds(mine + offset, 16), columns].astype(jnp.float32)
            total += from_core[batch, pl.ds(offset, 16), columns].astype(jnp.float32)
            pair_sum[batch, pl.ds(offset, 16), columns] = total.astype(jnp.bfloat16)
            return carry

        lax.fori_loop(0, 2 * ROWS // 16, step, 0)

    def owner_of(batch, index):
        even = token_tile(BATCHES[batch][index])
        odd = token_tile(BATCHES[batch][2 + index])
        return jnp.where(pair == 0, even, odd)

    def sum_copy(batch, index):
        owner = owner_of(batch, index)
        place = (chip - owner // 2 + 8) % 8 - 1
        place = jnp.maximum(place, 0)
        copy = pltpu.make_async_remote_copy(
            src_ref=pair_sum.at[batch, pl.ds(index * ROWS, ROWS)],
            dst_ref=arrived.at[place],
            send_sem=sum_send.at[batch, index],
            recv_sem=sum_recv.at[place],
            device_id=(row, owner),
            device_id_type=MESH,
        )
        return owner, copy

    pre_load.wait()
    take_and_forward(3)
    take_and_forward(5)
    wait_tile((1, 0))
    weight_load.wait()
    for batch in range(4):
        if batch == 1:
            for distance in (2, 6, 4, 1, 7):
                take_and_forward(distance)
            wait_tile((1, 3))
            wait_tile((1, 5))
        elif batch == 2:
            wait_tile((1, 2))
            wait_tile((1, 6))
        elif batch == 3:
            for distance in (4, 1, 7):
                wait_tile((1, distance))
        for half in range(HALVES):
            partial_half(batch, half)
            core_copy(batch, half).start()
        for slot in BATCHES[batch]:
            activate(slot)
        for half in range(HALVES):
            core_copy(batch, half).wait_recv()
            add_cores(batch, half)
        for index in range(2):
            owner, copy = sum_copy(batch, index)

            @pl.when(owner != col)
            def _():
                copy.start()

    def weight_step(i, carry):
        offset = pl.multiple_of(i * PIECE, PIECE)
        product = lax.dot_general(
            act[:, pl.ds(offset, PIECE)], tiles[...], (((0,), (0,)), ((), ())),
            preferred_element_type=jnp.float32,
        )
        grad_weight[pl.ds(offset, PIECE), :] = product.astype(jnp.bfloat16)
        return carry

    lax.fori_loop(0, HIDDEN // PIECE, weight_step, 0)

    own_batch, own_index = jnp.int32(0), jnp.int32(0)
    for batch in range(4):
        for index in range(2):
            here = owner_of(batch, index) == col
            own_batch = jnp.where(here, batch, own_batch)
            own_index = jnp.where(here, index, own_index)

    for place in range(7):
        pltpu.make_async_remote_copy(
            src_ref=arrived.at[place],
            dst_ref=arrived.at[place],
            send_sem=sum_send.at[0, 0],
            recv_sem=sum_recv.at[place],
            device_id=(row, partner_core),
            device_id_type=MESH,
        ).wait_recv()

    def finish(i, carry):
        offset = pl.multiple_of(i * 16, 16)
        total = pair_sum[own_batch, pl.ds(pl.multiple_of(own_index * ROWS + offset, 16), 16), :].astype(jnp.float32)
        for place in range(7):
            total += arrived[place, pl.ds(offset, 16), :].astype(jnp.float32)
        values = pre[pl.ds(pl.multiple_of(col * ROWS + offset, 16), 16), :].astype(jnp.float32)
        grad_pre[pl.ds(offset, 16), :] = (total * gelu_slope(values)).astype(jnp.bfloat16)
        return carry

    lax.fori_loop(0, ROWS // 16, finish, 0)

    for copy in sends:
        copy.wait_send()
    for batch in range(4):
        for half in range(HALVES):
            core_copy(batch, half).wait_send()
        for index in range(2):
            owner, copy = sum_copy(batch, index)

            @pl.when(owner != col)
            def _():
                copy.wait_send()


def body(grad_out, pre_act, weight):
    bf16 = jnp.bfloat16
    hbm = pl.BlockSpec(memory_space=pltpu.HBM)
    vmem = pl.BlockSpec(memory_space=pltpu.VMEM)
    dma = pltpu.SemaphoreType.DMA
    return pl.pallas_call(
        kernel,
        out_shape=(
            jax.ShapeDtypeStruct((ROWS, HIDDEN), bf16),
            jax.ShapeDtypeStruct((HIDDEN, WIDTH), bf16),
        ),
        in_specs=[hbm, hbm, hbm],
        out_specs=(vmem, vmem),
        scratch_shapes=[
            pltpu.VMEM((TOKENS, HIDDEN), bf16),
            pltpu.VMEM((HIDDEN, WIDTH), bf16),
            pltpu.VMEM((TOKENS, WIDTH), bf16),
            pltpu.VMEM((TOKENS, HIDDEN), bf16),
            pltpu.VMEM((TOKENS, HIDDEN), bf16),
            pltpu.VMEM((4, 2 * ROWS, HIDDEN), bf16),
            pltpu.VMEM((4, 2 * ROWS, HIDDEN), bf16),
            pltpu.VMEM((7, ROWS, HIDDEN), bf16),
            dma((3,)),
            dma((8,)),
            dma((16,)),
            dma((8,)),
            dma((4, HALVES)),
            dma((4, HALVES)),
            dma((4, 2)),
            dma((7,)),
        ],
        compiler_params=pltpu.CompilerParams(
            collective_id=0, has_side_effects=True, vmem_limit_bytes=62 * 10**6
        ),
        name="all_in_one",
    )(grad_out, pre_act, weight)


def solution(mesh):
    placed = (P("row", "col"), P(None, "row"), P("row", "col"))
    return jax.shard_map(
        body,
        mesh=mesh,
        in_specs=placed,
        out_specs=(P("col", "row"), P("row", "col")),
        check_vma=False,
    )
```

time: 349 us -> 64.3 us (0.18)
  the two profiles are of different devices: /device:TPU:2 before, /device:TPU:67 now
where the time goes in v1:
time: 64.3 us; the launch traced here: 64.1 us
  Pallas kernels  57.1 us (89%)
  local copies, waits for them, and re-layouts  6.44 us (10%)
    pallas_call x1, Pallas kernels, body(): pl.pallas_call(kernel, out_shape=(jax.ShapeDtypeStruct((ROWS, HIDDEN), bf...  57.1 us
    unnamed x2, local copies, waits for them, and re-layouts  6.44 us

profile of v1, /device:TPU:67, one launch (start us, length us, event | category | flops | bytes accessed | tf_op | source)
XLA Modules:
  0.0 64.1 jit_solution(623798065297371042)
XLA Ops:
  0.6 57.1 %all_in_one.1 = (bf16[32,3072]{1,0:T(8,128)(2,1)}, bf16[3072,768]{1,0:T(8,128)(2,1)}) custom-call(bf16[32,768]{1,0:T(8,128)(2,1)} %grad_out.1, bf16[512,3072]{1,0:T(8,128)(2,1)} %pre_act.1, bf16[3072,768]{1,0:T(8,128)(2,1)} %weight.1), custom_call_target="tpu_custom_call" | custom-call | tf_op jit(solution)/shard_map/all_in_one/pallas_call | solution.py:274
  57.7 1.6 %copy.7 = bf16[32,3072]{1,0:T(8,128)(2,1)} copy(bf16[32,3072]{1,0:T(8,128)(2,1)} %get-tuple-element.4) | data formatting | bytes 393216
  59.3 4.8 %copy.8 = bf16[3072,768]{1,0:T(8,128)(2,1)} copy(bf16[3072,768]{1,0:T(8,128)(2,1)} %get-tuple-element.5) | data formatting | bytes 9437184

commit v2 on v0

v2 whole, which is shorter than its diff:
```python
import jax
import jax.numpy as jnp
from jax import lax
from jax.experimental import pallas as pl
from jax.experimental.pallas import tpu as pltpu
from jax.sharding import PartitionSpec as P

MESH = pl.DeviceIdType.MESH
ROWS = 32
WIDTH = 768
HIDDEN = 3072
TOKENS = 512
HALF = HIDDEN // 2
FIRST, SECOND = pl.ds(0, HALF), pl.ds(HALF, HALF)

BATCHES = (
    ((0, 0), (1, 0), (0, 1), (0, 7)),
    ((0, 2), (0, 6), (1, 1), (1, 7)),
    ((1, 2), (1, 6), (0, 3), (0, 5)),
    ((0, 4), (1, 4), (1, 3), (1, 5)),
)
SLOTS = tuple(slot for batch in BATCHES for slot in batch)
INDEX = {slot: i for i, slot in enumerate(SLOTS)}


def gelu_value(values):
    inner = 0.7978845608 * (values + 0.044715 * values * values * values)
    return 0.5 * values * (1.0 + jnp.tanh(inner))


def gelu_slope(values):
    inner = 0.7978845608 * (values + 0.044715 * values * values * values)
    tanh_value = jnp.tanh(inner)
    return 0.5 * (1.0 + tanh_value) + 0.5 * values * (
        1.0 - tanh_value * tanh_value
    ) * 0.7978845608 * (1.0 + 3.0 * 0.044715 * values * values)


def kernel(
    grad_out, pre_act, weight, grad_pre, grad_weight,
    pre, wide, tiles, act, partial, from_core, pair_sum, xa, ya, yb, xb,
    load_sem, tile_send, tile_recv, core_send, core_recv,
    a_send, b_send, xa_recv, ya_recv, yb_recv, xb_send, xb_recv,
):
    row, col = lax.axis_index("row"), lax.axis_index("col")
    x_lo, z = row // 8, row % 8
    y, x_hi, core = col // 4, (col // 2) % 2, col % 2
    pair = (z + core) % 2

    def at_z(distance):
        return (x_lo * 8 + (z + distance) % 8, col)

    def at_y(there):
        return (row, there * 4 + x_hi * 2 + core)

    other_row = ((row + 8) % 16, col)
    other_core = (row, col + 1 - 2 * core)
    other_x = (row, col + 2 - 4 * x_hi)

    def token_tile(slot):
        other, distance = slot
        return ((x_lo + other) % 2) * 8 + (z + distance) % 8

    own_load = pltpu.make_async_copy(grad_out, tiles.at[pl.ds(0, ROWS)], load_sem.at[0])
    own_load.start()
    weight_load = pltpu.make_async_copy(weight, wide, load_sem.at[1])
    weight_load.start()
    pre_load = pltpu.make_async_copy(pre_act, pre, load_sem.at[2])
    pre_load.start()

    barrier = pltpu.get_barrier_semaphore()
    peers = [at_z(1), at_z(7), at_z(2), at_z(6), other_row, other_core, other_x]
    peers += [at_y((y + step) % 4) for step in (1, 2, 3)]
    for peer in peers:
        pl.semaphore_signal(barrier, inc=1, device_id=peer, device_id_type=MESH)
    own_load.wait()
    pl.semaphore_wait(barrier, len(peers))

    sends = []

    def remote(src, dst, send_sem, recv_sem, peer):
        return pltpu.make_async_remote_copy(
            src_ref=src, dst_ref=dst, send_sem=send_sem, recv_sem=recv_sem,
            device_id=peer, device_id_type=MESH,
        )

    def landed(dst, recv_sem):
        remote(dst, dst, tile_send.at[0], recv_sem, other_core).wait_recv()

    def part(slot, half=None):
        if half is None:
            return tiles.at[pl.ds(INDEX[slot] * ROWS, ROWS)]
        return tiles.at[pl.ds(INDEX[slot] * ROWS + half * 16, 16)]

    def tile_sem(slot, half):
        return tile_recv.at[INDEX[slot] if half != 1 else len(SLOTS)]

    def send_tile(source, landing, peer, half=None):
        copy = remote(
            part(source, half), part(landing, half), tile_send.at[len(sends)], tile_sem(landing, half), peer
        )
        copy.start()
        sends.append(copy)

    def wait_tile(slot, half=None):
        landed(part(slot, half), tile_sem(slot, half))

    def across(distance):
        send_tile((0, distance), (1, distance), other_row)

    def activate(slot):
        start = pl.multiple_of(token_tile(slot) * ROWS, ROWS)
        base = INDEX[slot] * ROWS

        def step(i, carry):
            offset = pl.multiple_of(i * 16, 16)
            values = pre[pl.ds(start + offset, 16), :].astype(jnp.float32)
            act[pl.ds(base + offset, 16), :] = gelu_value(values).astype(jnp.bfloat16)
            return carry

        lax.fori_loop(0, ROWS // 16, step, 0)

    def core_copy(batch, half):
        theirs = pl.multiple_of(batch * 4 * ROWS + (1 - pair) * 2 * ROWS, 2 * ROWS)
        columns = pl.ds(half * HALF, HALF)
        return remote(
            partial.at[pl.ds(theirs, 2 * ROWS), columns], from_core.at[batch, :, columns],
            core_send.at[batch, half], core_recv.at[batch, half], other_core,
        )

    def multiply(batch, half):
        rows = pl.ds(batch * 4 * ROWS, 4 * ROWS)
        columns = pl.ds(half * HALF, HALF)
        product = lax.dot_general(
            tiles[rows, :], wide[columns, :], (((1,), (1,)), ((), ())),
            preferred_element_type=jnp.float32,
        )
        partial[rows, columns] = product.astype(jnp.bfloat16)
        core_copy(batch, half).start()

    def add_cores(batch, half):
        mine = pl.multiple_of(batch * 4 * ROWS + pair * 2 * ROWS, 2 * ROWS)
        columns = pl.ds(half * HALF, HALF)
        landed(from_core.at[batch, :, columns], core_recv.at[batch, half])

        def step(i, carry):
            offset = pl.multiple_of(i * 16, 16)
            total = partial[pl.ds(mine + offset, 16), columns].astype(jnp.float32)
            total += from_core[batch, pl.ds(offset, 16), columns].astype(jnp.float32)
            pair_sum[batch, pl.ds(offset, 16), columns] = total.astype(jnp.bfloat16)
            return carry

        lax.fori_loop(0, 2 * ROWS // 16, step, 0)

    def owner_of(batch, index):
        even = token_tile(BATCHES[batch][index])
        odd = token_tile(BATCHES[batch][2 + index])
        return jnp.where(pair == 0, even, odd)

    def place_of(batch, index):
        owner = owner_of(batch, index)
        owner_y, owner_x = owner // 4, (owner // 2) % 2
        same_y, same_x = owner_y == y, owner_x == x_hi
        behind = jnp.maximum((y - owner_y + 4) % 4 - 1, 0)
        return owner_y, same_y, same_x, behind

    def x_first(batch, index):
        return remote(
            pair_sum.at[batch, pl.ds(index * ROWS, ROWS), FIRST], xa.at[batch, index],
            a_send.at[batch, index], xa_recv.at[batch, index], other_x,
        )

    def y_second(batch, index):
        owner_y, _, _, behind = place_of(batch, index)
        return remote(
            pair_sum.at[batch, pl.ds(index * ROWS, ROWS), FIRST], ya.at[behind],
            a_send.at[batch, index], ya_recv.at[behind], at_y(owner_y),
        )

    def y_first(batch, index):
        owner_y, _, same_x, behind = place_of(batch, index)
        side = jnp.where(same_x, 0, 1)
        return remote(
            pair_sum.at[batch, pl.ds(index * ROWS, ROWS), SECOND], yb.at[side, behind],
            b_send.at[batch, index], yb_recv.at[side, behind], at_y(owner_y),
        )

    def first_hops(batch, half):
        for index in range(2):
            _, same_y, same_x, _ = place_of(batch, index)
            if half == 0:

                @pl.when(jnp.logical_not(same_x))
                def _():
                    x_first(batch, index).start()

            else:

                @pl.when(jnp.logical_not(same_y))
                def _():
                    y_first(batch, index).start()

    def second_hops(batch):
        for index in range(2):
            _, same_y, same_x, _ = place_of(batch, index)

            @pl.when(same_x)
            def _():
                landed(xa.at[batch, index], xa_recv.at[batch, index])

                def step(i, carry):
                    offset = pl.multiple_of(i * 16, 16)
                    rows = pl.ds(index * ROWS + offset, 16)
                    total = pair_sum[batch, rows, FIRST].astype(jnp.float32)
                    total += xa[batch, index, pl.ds(offset, 16), :].astype(jnp.float32)
                    pair_sum[batch, rows, FIRST] = total.astype(jnp.bfloat16)
                    return carry

                lax.fori_loop(0, ROWS // 16, step, 0)

                @pl.when(jnp.logical_not(same_y))
                def _():
                    y_second(batch, index).start()

    def weight_part(half):
        columns = pl.ds(half * HALF, HALF)
        product = lax.dot_general(
            act[:, columns], tiles[...], (((0,), (0,)), ((), ())),
            preferred_element_type=jnp.float32,
        )
        grad_weight[columns, :] = product.astype(jnp.bfloat16)

    send_tile((0, 0), (1, 0), other_row)
    for distance in (1, 7, 2, 6):
        send_tile((0, 0), (0, 8 - distance), at_z(distance))
    pre_load.wait()
    for slot in SLOTS:
        activate(slot)
    wait_tile((0, 1))
    across(1)
    wait_tile((0, 7))
    across(7)
    wait_tile((1, 0))
    weight_load.wait()
    multiply(0, 0)
    wait_tile((0, 2))
    send_tile((0, 2), (0, 3), at_z(7))
    send_tile((0, 2), (0, 4), at_z(6), half=0)
    across(2)
    wait_tile((0, 6))
    send_tile((0, 6), (0, 5), at_z(1))
    send_tile((0, 6), (0, 4), at_z(2), half=1)
    across(6)
    multiply(0, 1)
    for half in range(2):
        add_cores(0, half)
        first_hops(0, half)

    wait_tile((1, 1))
    wait_tile((1, 7))
    multiply(1, 0)
    multiply(1, 1)
    wait_tile((0, 3))
    across(3)
    wait_tile((0, 5))
    across(5)
    wait_tile((0, 4), half=0)
    wait_tile((0, 4), half=1)
    across(4)
    for half in range(2):
        add_cores(1, half)
        first_hops(1, half)
    second_hops(0)

    wait_tile((1, 2))
    wait_tile((1, 6))
    multiply(2, 0)
    multiply(2, 1)
    for half in range(2):
        add_cores(2, half)
        first_hops(2, half)

    wait_tile((1, 3))
    wait_tile((1, 5))
    wait_tile((1, 4))
    multiply(3, 0)
    multiply(3, 1)
    second_hops(1)
    for half in range(2):
        add_cores(3, half)
        first_hops(3, half)
    second_hops(2)
    weight_part(0)
    second_hops(3)

    own_at, partner_at = jnp.int32(0), jnp.int32(0)
    for batch in range(4):
        for index in range(2):
            _, same_y, same_x, _ = place_of(batch, index)
            here = batch * 2 + index
            own_at = jnp.where(jnp.logical_and(same_y, same_x), here, own_at)
            partner_at = jnp.where(jnp.logical_and(same_y, jnp.logical_not(same_x)), here, partner_at)

    def held(at, offset, columns):
        start = pl.multiple_of((at % 2) * ROWS + offset, 16)
        return pair_sum[at // 2, pl.ds(start, 16), columns].astype(jnp.float32)

    for behind in range(3):
        landed(yb.at[1, behind], yb_recv.at[1, behind])

    def partner_step(i, carry):
        offset = pl.multiple_of(i * 16, 16)
        total = held(partner_at, offset, SECOND)
        for behind in range(3):
            total += yb[1, behind, pl.ds(offset, 16), :].astype(jnp.float32)
        xb[0, pl.ds(offset, 16), :] = total.astype(jnp.bfloat16)
        return carry

    lax.fori_loop(0, ROWS // 16, partner_step, 0)
    partner_copy = remote(xb.at[0], xb.at[1], xb_send.at[0], xb_recv.at[0], other_x)
    partner_copy.start()
    weight_part(1)

    for behind in range(3):
        landed(ya.at[behind], ya_recv.at[behind])
        landed(yb.at[0, behind], yb_recv.at[0, behind])

    def slope_at(offset, columns):
        start = pl.multiple_of(col * ROWS + offset, 16)
        return gelu_slope(pre[pl.ds(start, 16), columns].astype(jnp.float32))

    def first_step(i, carry):
        offset = pl.multiple_of(i * 16, 16)
        total = held(own_at, offset, FIRST)
        for behind in range(3):
            total += ya[behind, pl.ds(offset, 16), :].astype(jnp.float32)
        grad_pre[pl.ds(offset, 16), FIRST] = (total * slope_at(offset, FIRST)).astype(jnp.bfloat16)
        return carry

    lax.fori_loop(0, ROWS // 16, first_step, 0)
    landed(xb.at[1], xb_recv.at[0])

    def second_step(i, carry):
        offset = pl.multiple_of(i * 16, 16)
        total = held(own_at, offset, SECOND) + xb[1, pl.ds(offset, 16), :].astype(jnp.float32)
        for behind in range(3):
            total += yb[0, behind, pl.ds(offset, 16), :].astype(jnp.float32)
        grad_pre[pl.ds(offset, 16), SECOND] = (total * slope_at(offset, SECOND)).astype(jnp.bfloat16)
        return carry

    lax.fori_loop(0, ROWS // 16, second_step, 0)

    for copy in sends:
        copy.wait_send()
    partner_copy.wait_send()
    for batch in range(4):
        for half in range(2):
            core_copy(batch, half).wait_send()
        for index in range(2):
            _, same_y, same_x, _ = place_of(batch, index)

            @pl.when(jnp.logical_not(jnp.logical_and(same_x, same_y)))
            def _():
                x_first(batch, index).wait_send()

            @pl.when(jnp.logical_not(same_y))
            def _():
                y_first(batch, index).wait_send()


def write_out(grad_pre, grad_weight, grad_pre_out, grad_weight_out, sem):
    copies = [
        pltpu.make_async_copy(grad_weight, grad_weight_out, sem.at[0]),
        pltpu.make_async_copy(grad_pre, grad_pre_out, sem.at[1]),
    ]
    for copy in copies:
        copy.start()
    for copy in copies:
        copy.wait()


def body(grad_out, pre_act, weight):
    bf16 = jnp.bfloat16
    hbm = pl.BlockSpec(memory_space=pltpu.HBM)
    vmem = pl.BlockSpec(memory_space=pltpu.VMEM)
    dma = pltpu.SemaphoreType.DMA
    shapes = (
        jax.ShapeDtypeStruct((ROWS, HIDDEN), bf16),
        jax.ShapeDtypeStruct((HIDDEN, WIDTH), bf16),
    )
    held = (pltpu.VMEM((ROWS, HIDDEN), bf16), pltpu.VMEM((HIDDEN, WIDTH), bf16))
    args = [pltpu.with_memory_space_constraint(a, pltpu.HBM) for a in (grad_out, pre_act, weight)]
    grad_pre, grad_weight = pl.pallas_call(
        kernel,
        out_shape=held,
        in_specs=[hbm, hbm, hbm],
        out_specs=(vmem, vmem),
        scratch_shapes=[
            pltpu.VMEM((TOKENS, HIDDEN), bf16),
            pltpu.VMEM((HIDDEN, WIDTH), bf16),
            pltpu.VMEM((TOKENS, WIDTH), bf16),
            pltpu.VMEM((TOKENS, HIDDEN), bf16),
            pltpu.VMEM((TOKENS, HIDDEN), bf16),
            pltpu.VMEM((4, 2 * ROWS, HIDDEN), bf16),
            pltpu.VMEM((4, 2 * ROWS, HIDDEN), bf16),
            pltpu.VMEM((4, 2, ROWS, HALF), bf16),
            pltpu.VMEM((3, ROWS, HALF), bf16),
            pltpu.VMEM((2, 3, ROWS, HALF), bf16),
            pltpu.VMEM((2, ROWS, HALF), bf16),
            dma((3,)),
            dma((16,)),
            dma((17,)),
            dma((4, 2)),
            dma((4, 2)),
            dma((4, 2)),
            dma((4, 2)),
            dma((4, 2)),
            dma((3,)),
            dma((2, 3)),
            dma((1,)),
            dma((1,)),
        ],
        compiler_params=pltpu.CompilerParams(
            collective_id=0, has_side_effects=True, vmem_limit_bytes=40_000_000
        ),
        name="gather_multiply_sum",
    )(*args)
    return pl.pallas_call(
        write_out,
        out_shape=shapes,
        in_specs=[vmem, vmem],
        out_specs=(hbm, hbm),
        scratch_shapes=[dma((2,))],
        compiler_params=pltpu.CompilerParams(vmem_limit_bytes=2**20),
        name="write_out",
    )(
        pltpu.with_memory_space_constraint(grad_pre, pltpu.VMEM),
        pltpu.with_memory_space_constraint(grad_weight, pltpu.VMEM),
    )


def solution(mesh):
    placed = (P("row", "col"), P(None, "row"), P("row", "col"))
    return jax.shard_map(
        body,
        mesh=mesh,
        in_specs=placed,
        out_specs=(P("col", "row"), P("row", "col")),
        check_vma=False,
    )
```

time: 349 us -> 44.2 us (0.13)
  the two profiles are of different devices: /device:TPU:2 before, /device:TPU:46 now
where the time goes in v2:
time: 44.2 us
  Pallas kernels  43.5 us (98%)
  between operations  0.64 us (1%)
    pallas_call x1, Pallas kernels, body(): pl.pallas_call(kernel, out_shape=held, in_specs=[hbm, hbm, hbm], out_spec...  41.3 us
    pallas_call x1, Pallas kernels, body(): pl.pallas_call(write_out, out_shape=shapes, in_specs=[vmem, vmem], out_sp...  2.25 us

profile of v2, /device:TPU:46, one launch (start us, length us, event | category | flops | bytes accessed | tf_op | source)
XLA Modules:
  0.0 44.2 jit_solution(7569767844439112385)
XLA Ops:
  0.6 41.3 %gather_multiply_sum.1 = (bf16[32,3072]{1,0:T(8,128)(2,1)S(1)}, bf16[3072,768]{1,0:T(8,128)(2,1)S(1)}) custom-call(bf16[32,768]{1,0:T(8,128)(2,1)} %grad_out.1, bf16[512,3072]{1,0:T(8,128)(2,1)} %pre_act.1, bf16[3072,768]{1,0:T(8,128)(2,1)} %weight.1), custom_call_target="tpu_custom_call" | custom-call | tf_op jit(solution)/shard_map/gather_multiply_sum/pallas_call | solution.py:393
  41.9 2.2 %write_out.1 = (bf16[32,3072]{1,0:T(8,128)(2,1)}, bf16[3072,768]{1,0:T(8,128)(2,1)}) custom-call(bf16[32,3072]{1,0:T(8,128)(2,1)S(1)} %get-tuple-element.4.grad_pre, bf16[3072,768]{1,0:T(8,128)(2,1)S(1)} %get-tuple-element.5.grad_weight), custom_call_target="tpu_custom_call" | custom-call | tf_op jit(solution)/shard_map/write_out/pallas_call | solution.py:428

commit v3 on v2

v3 whole, which is shorter than its diff:
```python
import jax
import jax.numpy as jnp
from jax import lax
from jax.experimental import pallas as pl
from jax.experimental.pallas import tpu as pltpu
from jax.sharding import PartitionSpec as P

MESH = pl.DeviceIdType.MESH
ROWS = 32
WIDTH = 768
HIDDEN = 3072
TOKENS = 512
WIDTHS = (1536, 1536)
PARTS = (pl.ds(0, WIDTHS[0]), pl.ds(WIDTHS[0], WIDTHS[1]))
FIRST, SECOND = PARTS

BATCHES = (
    (((0, 0), (1, 0)), ((0, 1), (1, 7))),
    (((0, 2), (1, 6)), ((1, 1), (0, 7))),
    (((1, 2), (0, 6)), ((0, 3), (1, 5))),
    (((0, 4), (1, 4)), ((1, 3), (0, 5))),
)
SLOTS = tuple(slot for batch in BATCHES for group in batch for slot in group)
INDEX = {slot: i for i, slot in enumerate(SLOTS)}


def gelu_value(values):
    inner = 0.7978845608 * (values + 0.044715 * values * values * values)
    return 0.5 * values * (1.0 + jnp.tanh(inner))


def gelu_slope(values):
    inner = 0.7978845608 * (values + 0.044715 * values * values * values)
    tanh_value = jnp.tanh(inner)
    return 0.5 * (1.0 + tanh_value) + 0.5 * values * (
        1.0 - tanh_value * tanh_value
    ) * 0.7978845608 * (1.0 + 3.0 * 0.044715 * values * values)


def kernel(
    grad_out, pre_act, weight, grad_pre, grad_weight,
    pre, wide, tiles, act, partial, from_core, pair_sum, xa, ya, yb, xb, slope,
    load_sem, tile_send, tile_recv, core_send, core_recv,
    a_send, b_send, xa_recv, ya_recv, yb_recv, xb_send, xb_recv, ready,
):
    row, col = lax.axis_index("row"), lax.axis_index("col")
    x_lo, z = row // 8, row % 8
    y, x_hi, core = col // 4, (col // 2) % 2, col % 2
    pair = (z + core) % 2

    def at_z(distance):
        return (x_lo * 8 + (z + distance) % 8, col)

    def diagonal(distance):
        return ((1 - x_lo) * 8 + (z + distance) % 8, col)

    def at_y(there):
        return (row, there * 4 + x_hi * 2 + core)

    other_row = ((row + 8) % 16, col)
    other_core = (row, col + 1 - 2 * core)
    other_x = (row, col + 2 - 4 * x_hi)

    def token_tile(slot):
        other, distance = slot
        return ((x_lo + other) % 2) * 8 + (z + distance) % 8

    own_load = pltpu.make_async_copy(grad_out, tiles.at[pl.ds(0, ROWS)], load_sem.at[0])
    own_load.start()
    pre_load = pltpu.make_async_copy(pre_act, pre, load_sem.at[2])
    pre_load.start()
    weight_load = pltpu.make_async_copy(weight, wide, load_sem.at[1])
    weight_load.start()

    barrier = pltpu.get_barrier_semaphore()
    peers = [at_z(d) for d in (1, 7, 2, 6)] + [diagonal(d) for d in (1, 7, 2, 6)]
    peers += [other_row, other_core]
    for peer in peers:
        pl.semaphore_signal(barrier, inc=1, device_id=peer, device_id_type=MESH)

    @pl.when(x_hi == 0)
    def _():
        pl.semaphore_signal(barrier, inc=1, device_id=other_x, device_id_type=MESH)

    for there in range(1, 4):

        @pl.when(there > y)
        def _():
            pl.semaphore_signal(barrier, inc=1, device_id=at_y(there), device_id_type=MESH)

    pl.semaphore_wait(barrier, len(peers) + x_hi + y)

    sends = []

    def remote(src, dst, send_sem, recv_sem, peer):
        return pltpu.make_async_remote_copy(
            src_ref=src, dst_ref=dst, send_sem=send_sem, recv_sem=recv_sem,
            device_id=peer, device_id_type=MESH,
        )

    def landed(dst, recv_sem):
        remote(dst, dst, tile_send.at[0], recv_sem, other_core).wait_recv()

    def part(slot):
        return tiles.at[pl.ds(INDEX[slot] * ROWS, ROWS)]

    def send_tile(source, landing, peer):
        copy = remote(
            grad_out if source == (0, 0) else part(source), part(landing),
            tile_send.at[len(sends)], tile_recv.at[INDEX[landing]], peer,
        )
        copy.start()
        sends.append(copy)

    def wait_tile(slot):
        landed(part(slot), tile_recv.at[INDEX[slot]])

    def across(slot):
        send_tile(slot, (1 - slot[0], slot[1]), other_row)

    def activate(slot):
        start = pl.multiple_of(token_tile(slot) * ROWS, ROWS)
        base = INDEX[slot] * ROWS

        def step(i, carry):
            offset = pl.multiple_of(i * 16, 16)
            values = pre[pl.ds(start + offset, 16), :].astype(jnp.float32)
            act[pl.ds(base + offset, 16), :] = gelu_value(values).astype(jnp.bfloat16)
            return carry

        lax.fori_loop(0, ROWS // 16, step, 0)

    def groups(batch):
        for parity, slots in enumerate(BATCHES[batch]):
            if slots:
                yield parity, slots, pl.ds(INDEX[slots[0]] * ROWS, len(slots) * ROWS)

    def core_copy(batch, parity, rows, part):
        return remote(
            partial.at[rows, PARTS[part]], from_core.at[rows, PARTS[part]],
            core_send.at[batch, parity, part], core_recv.at[batch, parity, part], other_core,
        )

    def multiply(batch, part):
        slots = BATCHES[batch][0] + BATCHES[batch][1]
        every = pl.ds(INDEX[slots[0]] * ROWS, len(slots) * ROWS)
        columns = PARTS[part]
        product = lax.dot_general(
            tiles[every, :], wide[columns, :], (((1,), (1,)), ((), ())),
            preferred_element_type=jnp.float32,
        )
        partial[every, columns] = product.astype(jnp.bfloat16)
        for parity, _, rows in groups(batch):

            @pl.when(pair != parity)
            def _():
                core_copy(batch, parity, rows, part).start()

    def place_of(slot):
        owner = token_tile(slot)
        owner_y, owner_x = owner // 4, (owner // 2) % 2
        same_y, same_x = owner_y == y, owner_x == x_hi
        behind = jnp.maximum((y - owner_y + 4) % 4 - 1, 0)
        return owner_y, same_y, same_x, behind

    def slot_rows(slot):
        return pl.ds(INDEX[slot] * ROWS, ROWS)

    def x_first(slot):
        i = INDEX[slot]
        return remote(
            pair_sum.at[slot_rows(slot), FIRST], xa.at[i], a_send.at[i], xa_recv.at[i], other_x
        )

    def y_second(slot):
        owner_y, _, _, behind = place_of(slot)
        return remote(
            pair_sum.at[slot_rows(slot), FIRST], ya.at[behind],
            a_send.at[INDEX[slot]], ya_recv.at[behind], at_y(owner_y),
        )

    def y_first(slot):
        owner_y, _, same_x, behind = place_of(slot)
        side = jnp.where(same_x, 0, 1)
        return remote(
            pair_sum.at[slot_rows(slot), SECOND], yb.at[side, behind],
            b_send.at[INDEX[slot]], yb_recv.at[side, behind], at_y(owner_y),
        )

    def first_hops(batch, part):
        columns = PARTS[part]
        for parity, slots, rows in groups(batch):

            @pl.when(pair == parity)
            def _():
                landed(from_core.at[rows, columns], core_recv.at[batch, parity, part])
                for slot in slots:

                    def step(i, carry):
                        at = pl.ds(pl.multiple_of(INDEX[slot] * ROWS + i * 16, 16), 16)
                        total = partial[at, columns].astype(jnp.float32)
                        total += from_core[at, columns].astype(jnp.float32)
                        pair_sum[at, columns] = total.astype(jnp.bfloat16)
                        return carry

                    lax.fori_loop(0, ROWS // 16, step, 0)
                    _, same_y, same_x, _ = place_of(slot)
                    if part == 0:

                        @pl.when(jnp.logical_not(same_x))
                        def _():
                            x_first(slot).start()

                    else:

                        @pl.when(jnp.logical_not(same_y))
                        def _():
                            y_first(slot).start()

    def second_hops(batch):
        for parity, slots, _ in groups(batch):
            for slot in slots:
                _, same_y, same_x, _ = place_of(slot)
                i = INDEX[slot]

                @pl.when(jnp.logical_and(pair == parity, same_x))
                def _():
                    landed(xa.at[i], xa_recv.at[i])

                    def step(j, carry):
                        offset = pl.multiple_of(j * 16, 16)
                        at = pl.ds(i * ROWS + offset, 16)
                        total = pair_sum[at, FIRST].astype(jnp.float32)
                        total += xa[i, pl.ds(offset, 16), :].astype(jnp.float32)
                        pair_sum[at, FIRST] = total.astype(jnp.bfloat16)
                        return carry

                    lax.fori_loop(0, ROWS // 16, step, 0)

                    @pl.when(jnp.logical_not(same_y))
                    def _():
                        y_second(slot).start()

    def find_slope():
        def step(i, carry):
            offset = pl.multiple_of(i * 16, 16)
            values = pre[pl.ds(pl.multiple_of(col * ROWS + offset, 16), 16), :].astype(jnp.float32)
            slope[pl.ds(offset, 16), :] = gelu_slope(values)
            return carry

        lax.fori_loop(0, ROWS // 16, step, 0)

    def weight_part(part):
        columns = PARTS[part]
        product = lax.dot_general(
            act[:, columns], tiles[...], (((0,), (0,)), ((), ())),
            preferred_element_type=jnp.float32,
        )
        grad_weight[columns, :] = product.astype(jnp.bfloat16)

    send_tile((0, 0), (1, 0), other_row)
    send_tile((0, 0), (0, 1), at_z(7))
    send_tile((0, 0), (1, 7), diagonal(1))
    send_tile((0, 0), (0, 2), at_z(6))
    send_tile((0, 0), (1, 6), diagonal(2))

    @pl.when(x_hi == 1)
    def _():
        pl.semaphore_signal(ready, inc=1, device_id=other_x, device_id_type=MESH)

    for there in range(3):

        @pl.when(there < y)
        def _():
            pl.semaphore_signal(ready, inc=1, device_id=at_y(there), device_id_type=MESH)

    pre_load.wait()
    for slot in SLOTS:
        activate(slot)
    for slot in ((0, 1), (1, 7)):
        wait_tile(slot)
        across(slot)
    own_load.wait()
    weight_load.wait()
    wait_tile((1, 0))
    multiply(0, 0)
    wait_tile((0, 2))
    send_tile((0, 2), (0, 3), at_z(7))
    send_tile((0, 2), (0, 4), at_z(6))
    across((0, 2))
    wait_tile((1, 6))
    send_tile((1, 6), (1, 5), at_z(1))
    send_tile((1, 6), (1, 4), at_z(2))
    across((1, 6))
    multiply(0, 1)
    find_slope()
    for count in range(1, 5):

        @pl.when(4 - x_hi - y == count)
        def _():
            pl.semaphore_wait(ready, count)

    first_hops(0, 0)
    first_hops(0, 1)

    for slot in ((1, 1), (0, 7)):
        wait_tile(slot)
    multiply(1, 0)
    multiply(1, 1)
    for slot in ((0, 3), (1, 5)):
        wait_tile(slot)
        across(slot)
    first_hops(1, 0)
    first_hops(1, 1)
    second_hops(0)

    for slot in ((1, 2), (0, 6)):
        wait_tile(slot)
    multiply(2, 0)
    multiply(2, 1)
    first_hops(2, 0)
    first_hops(2, 1)

    for slot in ((0, 4), (1, 4), (1, 3), (0, 5)):
        wait_tile(slot)
    multiply(3, 0)
    multiply(3, 1)
    second_hops(1)
    first_hops(3, 0)
    first_hops(3, 1)
    second_hops(2)
    weight_part(0)
    second_hops(3)

    own_at, partner_at = jnp.int32(0), jnp.int32(0)
    for slot in SLOTS:
        own_at = jnp.where(token_tile(slot) == col, INDEX[slot], own_at)
        partner_at = jnp.where(token_tile(slot) == other_x[1], INDEX[slot], partner_at)

    def held(at, offset, columns):
        start = pl.multiple_of(at * ROWS + offset, 16)
        return pair_sum[pl.ds(start, 16), columns].astype(jnp.float32)

    for behind in range(3):
        landed(yb.at[1, behind], yb_recv.at[1, behind])

    def partner_step(i, carry):
        offset = pl.multiple_of(i * 16, 16)
        total = held(partner_at, offset, SECOND)
        for behind in range(3):
            total += yb[1, behind, pl.ds(offset, 16), :].astype(jnp.float32)
        xb[0, pl.ds(offset, 16), :] = total.astype(jnp.bfloat16)
        return carry

    lax.fori_loop(0, ROWS // 16, partner_step, 0)
    partner_copy = remote(xb.at[0], xb.at[1], xb_send.at[0], xb_recv.at[0], other_x)
    partner_copy.start()
    weight_part(1)

    for behind in range(3):
        landed(ya.at[behind], ya_recv.at[behind])
        landed(yb.at[0, behind], yb_recv.at[0, behind])

    def first_step(i, carry):
        offset = pl.multiple_of(i * 16, 16)
        total = held(own_at, offset, FIRST)
        for behind in range(3):
            total += ya[behind, pl.ds(offset, 16), :].astype(jnp.float32)
        grad_pre[pl.ds(offset, 16), FIRST] = (total * slope[pl.ds(offset, 16), FIRST]).astype(jnp.bfloat16)
        return carry

    lax.fori_loop(0, ROWS // 16, first_step, 0)
    landed(xb.at[1], xb_recv.at[0])

    def second_step(i, carry):
        offset = pl.multiple_of(i * 16, 16)
        total = held(own_at, offset, SECOND) + xb[1, pl.ds(offset, 16), :].astype(jnp.float32)
        for behind in range(3):
            total += yb[0, behind, pl.ds(offset, 16), :].astype(jnp.float32)
        grad_pre[pl.ds(offset, 16), SECOND] = (total * slope[pl.ds(offset, 16), SECOND]).astype(jnp.bfloat16)
        return carry

    lax.fori_loop(0, ROWS // 16, second_step, 0)

    for copy in sends:
        copy.wait_send()
    partner_copy.wait_send()
    for batch in range(len(BATCHES)):
        for parity, slots, rows in groups(batch):

            @pl.when(pair != parity)
            def _():
                for part in range(2):
                    core_copy(batch, parity, rows, part).wait_send()

            for slot in slots:
                _, same_y, same_x, _ = place_of(slot)
                mine = pair == parity

                @pl.when(jnp.logical_and(mine, jnp.logical_not(jnp.logical_and(same_x, same_y))))
                def _():
                    x_first(slot).wait_send()

                @pl.when(jnp.logical_and(mine, jnp.logical_not(same_y)))
                def _():
                    y_first(slot).wait_send()


def write_out(grad_pre, grad_weight, grad_pre_out, grad_weight_out, sem):
    copies = [
        pltpu.make_async_copy(grad_weight, grad_weight_out, sem.at[0]),
        pltpu.make_async_copy(grad_pre, grad_pre_out, sem.at[1]),
    ]
    for copy in copies:
        copy.start()
    for copy in copies:
        copy.wait()


def body(grad_out, pre_act, weight):
    bf16 = jnp.bfloat16
    hbm = pl.BlockSpec(memory_space=pltpu.HBM)
    vmem = pl.BlockSpec(memory_space=pltpu.VMEM)
    dma = pltpu.SemaphoreType.DMA
    shapes = (
        jax.ShapeDtypeStruct((ROWS, HIDDEN), bf16),
        jax.ShapeDtypeStruct((HIDDEN, WIDTH), bf16),
    )
    held = (pltpu.VMEM((ROWS, HIDDEN), bf16), pltpu.VMEM((HIDDEN, WIDTH), bf16))
    args = [pltpu.with_memory_space_constraint(a, pltpu.HBM) for a in (grad_out, pre_act, weight)]
    grad_pre, grad_weight = pl.pallas_call(
        kernel,
        out_shape=held,
        in_specs=[hbm, hbm, hbm],
        out_specs=(vmem, vmem),
        scratch_shapes=[
            pltpu.VMEM((TOKENS, HIDDEN), bf16),
            pltpu.VMEM((HIDDEN, WIDTH), bf16),
            pltpu.VMEM((TOKENS, WIDTH), bf16),
            pltpu.VMEM((TOKENS, HIDDEN), bf16),
            pltpu.VMEM((TOKENS, HIDDEN), bf16),
            pltpu.VMEM((TOKENS, HIDDEN), bf16),
            pltpu.VMEM((TOKENS, HIDDEN), bf16),
            pltpu.VMEM((16, ROWS, WIDTHS[0]), bf16),
            pltpu.VMEM((3, ROWS, WIDTHS[0]), bf16),
            pltpu.VMEM((2, 3, ROWS, WIDTHS[1]), bf16),
            pltpu.VMEM((2, ROWS, WIDTHS[1]), bf16),
            pltpu.VMEM((ROWS, HIDDEN), jnp.float32),
            dma((3,)),
            dma((16,)),
            dma((16,)),
            dma((4, 2, 2)),
            dma((4, 2, 2)),
            dma((16,)),
            dma((16,)),
            dma((16,)),
            dma((3,)),
            dma((2, 3)),
            dma((1,)),
            dma((1,)),
            pltpu.SemaphoreType.REGULAR,
        ],
        compiler_params=pltpu.CompilerParams(
            collective_id=0, has_side_effects=True, vmem_limit_bytes=40_000_000
        ),
        name="gather_multiply_sum",
    )(*args)
    return pl.pallas_call(
        write_out,
        out_shape=shapes,
        in_specs=[vmem, vmem],
        out_specs=(hbm, hbm),
        scratch_shapes=[dma((2,))],
        compiler_params=pltpu.CompilerParams(vmem_limit_bytes=2**20),
        name="write_out",
    )(
        pltpu.with_memory_space_constraint(grad_pre, pltpu.VMEM),
        pltpu.with_memory_space_constraint(grad_weight, pltpu.VMEM),
    )


def solution(mesh):
    placed = (P("row", "col"), P(None, "row"), P("row", "col"))
    return jax.shard_map(
        body,
        mesh=mesh,
        in_specs=placed,
        out_specs=(P("col", "row"), P("row", "col")),
        check_vma=False,
    )
```

time: 44.2 us -> 44.2 us (level)
  the two profiles are of different devices: /device:TPU:46 before, /device:TPU:44 now
where the time goes in v3:
time: 44.2 us; the launch traced here: 44.1 us
  Pallas kernels  43.4 us (98%)
  between operations  0.64 us (1%)
    pallas_call x1, Pallas kernels, body(): pl.pallas_call(kernel, out_shape=held, in_specs=[hbm, hbm, hbm], out_spec...  41.2 us
    pallas_call x1, Pallas kernels, body(): pl.pallas_call(write_out, out_shape=shapes, in_specs=[vmem, vmem], out_sp...  2.25 us

profile of v3, /device:TPU:44, one launch (start us, length us, event | category | flops | bytes accessed | tf_op | source)
XLA Modules:
  0.0 44.1 jit_solution(12519679731101233528)
XLA Ops:
  0.6 41.2 %gather_multiply_sum.1 = (bf16[32,3072]{1,0:T(8,128)(2,1)S(1)}, bf16[3072,768]{1,0:T(8,128)(2,1)S(1)}) custom-call(bf16[32,768]{1,0:T(8,128)(2,1)} %grad_out.1, bf16[512,3072]{1,0:T(8,128)(2,1)} %pre_act.1, bf16[3072,768]{1,0:T(8,128)(2,1)} %weight.1), custom_call_target="tpu_custom_call" | custom-call | tf_op jit(solution)/shard_map/gather_multiply_sum/pallas_call | solution.py:431
  41.8 2.2 %write_out.1 = (bf16[32,3072]{1,0:T(8,128)(2,1)}, bf16[3072,768]{1,0:T(8,128)(2,1)}) custom-call(bf16[32,3072]{1,0:T(8,128)(2,1)S(1)} %get-tuple-element.4.grad_pre, bf16[3072,768]{1,0:T(8,128)(2,1)S(1)} %get-tuple-element.5.grad_weight), custom_call_target="tpu_custom_call" | custom-call | tf_op jit(solution)/shard_map/write_out/pallas_call | solution.py:468
